TPU v7x, 32 devices: a whole 2x2x4 slice. The times are simulated.
32 devices in a mesh: wide: 8 (over y, x, core), narrow: 4 (over z).
Axes of the slice: x: 2, y: 2, z: 4, core: 2. Of those that a mesh axis runs over, the one named last changes fastest.
Arguments:
- amplitude: float32 [2048, 256], P(('wide', 'narrow')), may hold values from -6 to 6
- tilt: float32 [3, 2048], P(None, ('wide', 'narrow')), may hold values from -3.140625 to 3.140625
- owner: int32 [2048, 1], P(('wide', 'narrow')), may hold values from 0 to 7; in each aligned block of 64 rows (0 to 63, 64 to 127, ...) at most 24 rows name the same one
- row_offset: int32 [2048], P(('wide', 'narrow')), may hold values from 0 to 496
- col_offset: int32 [2048], P(('wide', 'narrow')), may hold values from 0 to 240
Outputs:
- hologram: float32 [2, 2048, 2048], P(None, 'narrow', 'wide')
Inputs may be any that keep to these rules, and one draw needn't show every extreme that they name: `owner`: among the 64 facets of one device no tile column is named more than 24 times, and on some device one column is named exactly 24 times.
All inputs are finite; a program needn't handle non-finite values.
Results may differ from a plain program's by a relative error of at most 0.0085.
Values may be sent and summed in bfloat16 or wider, within the bound.
A program may use at most 64 MiB of HBM per device.

v0:
```python
import math

import jax
import jax.numpy as jnp
from jax import lax
from jax.sharding import PartitionSpec as P

TH = 512
TW = 256
FACET = 16
DEPTH = 1280


reach_spread = 16.0


def from_behind(value, axis, steps):
    count = lax.axis_size(axis)
    leading, last = (max(0, -steps), min(count, count - steps))
    return lax.ppermute(value, axis, [(source, source + steps) for source in range(leading, last)])


def dft_tables(length, spin_sign):
    position = jnp.arange(length, dtype=jnp.int32)
    product = position[:, None] * position[None, :] % length
    angles = product.astype(jnp.float32) * (2.0 * math.pi / length)
    return (
        jnp.cos(angles).astype(jnp.bfloat16),
        (spin_sign * jnp.sin(angles)).astype(jnp.bfloat16),
    )


def signed_frequency(length):
    position = jnp.arange(length, dtype=jnp.int32)
    return (position + length // 2) % length - length // 2


def reach_weight(length, depth_cells, offset):
    travel = signed_frequency(length).astype(jnp.float32) * (depth_cells / (length * length))
    return jnp.exp(-((travel - offset) ** 2) / reach_spread)


def depth_phase(length, depth_cells):
    frequency = signed_frequency(length)
    turn_count = depth_cells * frequency * frequency % (2 * length * length)
    return turn_count.astype(jnp.float32) * (-math.pi / (length * length))


def render(amplitude, tilt, patch):
    position = jnp.arange(patch * patch, dtype=jnp.int32)
    row_pos = (position // patch).astype(jnp.float32)
    col_pos = (position % patch).astype(jnp.float32)
    phase = (
        tilt[0][:, None] * row_pos[None, :] + tilt[1][:, None] * col_pos[None, :] + tilt[2][:, None]
    )
    return (
        (amplitude * jnp.cos(phase)).astype(jnp.bfloat16),
        (amplitude * jnp.sin(phase)).astype(jnp.bfloat16),
    )


def left_apply(table_r, table_i, real_part, imag_part):
    real_real = jnp.dot(table_r, real_part, preferred_element_type=jnp.float32)
    imag_imag = jnp.dot(table_i, imag_part, preferred_element_type=jnp.float32)
    real_imag = jnp.dot(table_r, imag_part, preferred_element_type=jnp.float32)
    imag_real = jnp.dot(table_i, real_part, preferred_element_type=jnp.float32)
    return (real_real - imag_imag, real_imag + imag_real)


def right_apply(real_part, imag_part, table_r, table_i):
    real_real = jnp.dot(real_part, table_r, preferred_element_type=jnp.float32)
    imag_imag = jnp.dot(imag_part, table_i, preferred_element_type=jnp.float32)
    real_imag = jnp.dot(real_part, table_i, preferred_element_type=jnp.float32)
    imag_real = jnp.dot(imag_part, table_r, preferred_element_type=jnp.float32)
    return (real_real - imag_imag, real_imag + imag_real)


def wide_terms(spectrum):
    found = []
    for offset in (-2, -1, 1, 2):
        found.append((offset, from_behind(spectrum, "wide", offset)))
    return found


def narrow_terms(column_sum):
    found = []
    for offset in (-2, -1, 1, 2):
        found.append((offset, from_behind(column_sum, "narrow", offset)))
    return found


def local(amplitude, tilt, owner, row_offset, col_offset):
    wide_count = lax.axis_size("wide")
    facet_count = amplitude.shape[0]
    slot_count = max(2, (3 * facet_count + wide_count - 1) // wide_count)
    total_slots = wide_count * slot_count
    field_r, field_i = render(amplitude, tilt, FACET)
    packed = jnp.concatenate([field_r, field_i], axis=1)
    target = owner[:, 0]
    columns = jnp.arange(wide_count, dtype=jnp.int32)
    chosen = (target[:, None] == columns[None, :]).astype(jnp.int32)
    earlier = jnp.cumsum(chosen, axis=0) - chosen
    rank_in = jnp.sum(earlier * chosen, axis=1)
    slot_at = target * slot_count + rank_in
    outgoing = jnp.zeros((total_slots, 2 * FACET * FACET), jnp.bfloat16).at[slot_at].set(packed)
    corners = jnp.stack([row_offset, col_offset], axis=1)
    corner_out = jnp.zeros((total_slots, 2), jnp.int32).at[slot_at].set(corners)
    incoming, corner_in = (
        lax.all_to_all(
            outgoing.reshape(wide_count, slot_count, 2 * FACET * FACET),
            "wide",
            split_axis=0,
            concat_axis=0,
            tiled=True,
        ),
        lax.all_to_all(
            corner_out.reshape(wide_count, slot_count, 2),
            "wide",
            split_axis=0,
            concat_axis=0,
            tiled=True,
        ),
    )
    fields = incoming.reshape(total_slots, 2, FACET, FACET)
    corner_in = corner_in.reshape(total_slots, 2)
    pixel = jnp.arange(FACET, dtype=jnp.int32)
    col_hot = (
        jnp.arange(TW, dtype=jnp.int32)[None, None, :]
        == corner_in[:, 1][:, None, None] + pixel[None, :, None]
    ).astype(jnp.bfloat16)
    spread = jnp.einsum(
        "scuv,svx->sucx", fields, col_hot, preferred_element_type=jnp.float32
    ).astype(jnp.bfloat16)
    row_hot = (
        jnp.arange(TH, dtype=jnp.int32)[:, None, None]
        == corner_in[:, 0][None, :, None] + pixel[None, None, :]
    ).astype(jnp.bfloat16)
    plane = jnp.dot(
        row_hot.reshape(TH, total_slots * FACET),
        spread.reshape(total_slots * FACET, 2 * TW),
        preferred_element_type=jnp.float32,
    )
    wrp_r = plane[:, :TW].astype(jnp.bfloat16)
    wrp_i = plane[:, TW:].astype(jnp.bfloat16)
    fwd_hr, fwd_hi = dft_tables(TH, -1.0)
    fwd_wr, fwd_wi = dft_tables(TW, -1.0)
    inv_hr, inv_hi = dft_tables(TH, 1.0)
    inv_wr, inv_wi = dft_tables(TW, 1.0)
    scale = 1.0 / math.sqrt(TH * TW)
    rows_r, rows_i = left_apply(fwd_hr, fwd_hi, wrp_r, wrp_i)
    spec_r, spec_i = right_apply(
        rows_r.astype(jnp.bfloat16), rows_i.astype(jnp.bfloat16), fwd_wr, fwd_wi
    )
    spectrum = jnp.stack(
        [(spec_r * scale).astype(jnp.bfloat16), (spec_i * scale).astype(jnp.bfloat16)]
    )
    col_total = reach_weight(TW, DEPTH, 0.0)[None, None, :] * spectrum.astype(jnp.float32)
    for offset, piece in wide_terms(spectrum):
        col_total = col_total + reach_weight(TW, DEPTH, float(offset))[
            None, None, :
        ] * piece.astype(jnp.float32)
    column_sum = col_total.astype(jnp.bfloat16)
    band_total = reach_weight(TH, DEPTH, 0.0)[None, :, None] * column_sum.astype(jnp.float32)
    for offset, piece in narrow_terms(column_sum):
        band_total = band_total + reach_weight(TH, DEPTH, float(offset))[
            None, :, None
        ] * piece.astype(jnp.float32)
    angle = depth_phase(TH, DEPTH)[:, None] + depth_phase(TW, DEPTH)[None, :]
    phase_r = jnp.cos(angle)
    phase_i = jnp.sin(angle)
    focus_r = (phase_r * band_total[0] - phase_i * band_total[1]).astype(jnp.bfloat16)
    focus_i = (phase_r * band_total[1] + phase_i * band_total[0]).astype(jnp.bfloat16)
    cols_r, cols_i = right_apply(focus_r, focus_i, inv_wr, inv_wi)
    out_r, out_i = left_apply(
        inv_hr, inv_hi, cols_r.astype(jnp.bfloat16), cols_i.astype(jnp.bfloat16)
    )
    return jnp.stack([out_r * scale, out_i * scale])


def solution(mesh):
    in_specs = (
        P(("wide", "narrow"), None),
        P(None, ("wide", "narrow")),
        P(("wide", "narrow"), None),
        P(("wide", "narrow")),
        P(("wide", "narrow")),
    )
    out_specs = P(None, "narrow", "wide")
    return jax.shard_map(local, mesh=mesh, in_specs=in_specs, out_specs=out_specs, check_vma=False)
```

profile of v0, /device:TPU:28, one launch (start us, length us, event | category | flops | bytes accessed | tf_op | source)
XLA Modules:
  0.0 160.5 jit_solution(13914676809886142409)
XLA Ops:
  4.6 4.2 %all-to-all-start = ((s32[8,24,2]{1,2,0:T(2,128)}), s32[8,24,2]{1,2,0:T(2,128)S(1)}, u32[]{:S(2)}, u32[]{:S(2)}) async-start(s32[8,24,2]{1,2,0:T(2,128)} %copy.17), calls=%async_computation | async-start | bytes 16384 | tf_op jit(solution)/shard_map/all_to_all | solution.py:116
  10.9 1.5 scatter_custom_fusion.1
  12.4 4.4 %all-to-all-start.1 = ((bf16[8,24,512]{2,1,0:T(8,128)(2,1)}), bf16[8,24,512]{2,1,0:T(8,128)(2,1)S(1)}, u32[]{:S(2)}, u32[]{:S(2)}) async-start(bf16[8,24,512]{2,1,0:T(8,128)(2,1)} %bitcast.13), calls=%async_computation.1 | async-start | bytes 393216 | tf_op jit(solution)/shard_map/all_to_all | solution.py:109
  17.2 4.4 %all-to-all-done.1 = bf16[8,24,512]{2,1,0:T(8,128)(2,1)S(1)} async-done(((bf16[8,24,512]{2,1,0:T(8,128)(2,1)}), bf16[8,24,512]{2,1,0:T(8,128)(2,1)S(1)}, u32[]{:S(2)}, u32[]{:S(2)}) %all-to-all-start.1) | async-done | bytes 196640 | tf_op jit(solution)/shard_map/all_to_all | solution.py:109
  21.6 1.3 reshape.282
  22.9 1.5 convert_bitcast_fusion
  24.4 3.2 %copy.21 = bf16[192,16,2,256]{3,2,1,0:T(2,128)(2,1)S(1)} copy(bf16[192,16,2,256]{3,1,2,0:T(8,128)(2,1)S(1)} %convert_bitcast_fusion) | data formatting | bytes 6291456 | tf_op jit(solution)/shard_map/convert_element_type | solution.py:133
  28.3 1.8 %fusion.8 = bf16[512,512]{1,0:T(8,128)(2,1)S(1)} fusion(bf16[3072,512]{1,0:T(8,128)(2,1)S(1)} %bitcast.70, s32[3072]{0:T(1024)S(1)} %add.507), kind=kOutput, calls=%fused_computation.13 | convolution fusion | flops 1612447744 | bytes 3682304 | tf_op jit(solution)/shard_map/dot_general | solution.py:138
  30.1 4.0 %fusion.41 = f32[512,256]{1,0:T(8,128)S(1)} fusion(bf16[512,512]{1,0:T(8,128)(2,1)S(1)} %fusion.8), kind=kOutput, calls=%fused_computation.64 | convolution fusion | flops 138149888 | bytes 786432 | tf_op jit(solution)/shard_map/dot_general | solution.py:65
  34.1 4.2 %fusion.42 = f32[512,256]{1,0:T(8,128)S(1)} fusion(bf16[512,512]{1,0:T(8,128)(2,1)S(1)} %fusion.8), kind=kOutput, calls=%fused_computation.65 | convolution fusion | flops 138149888 | bytes 786432 | tf_op jit(solution)/shard_map/dot_general | solution.py:63
  38.3 4.2 %fusion.15 = bf16[512,256]{1,0:T(8,128)(2,1)S(1)} fusion(f32[512,256]{1,0:T(8,128)S(1)} %fusion.42, bf16[512,512]{1,0:T(8,128)(2,1)S(1)} %fusion.8), kind=kOutput, calls=%fused_computation.28 | convolution fusion | flops 138674176 | bytes 1048576 | tf_op jit(solution)/shard_map/dot_general | solution.py:64
  44.8 4.2 %fusion.16 = bf16[512,256]{1,0:T(8,128)(2,1)S(1)} fusion(f32[512,256]{1,0:T(8,128)S(1)} %fusion.41, bf16[512,512]{1,0:T(8,128)(2,1)S(1)} %fusion.8), kind=kOutput, calls=%fused_computation.29 | convolution fusion | flops 138674176 | bytes 1048576 | tf_op jit(solution)/shard_map/dot_general | solution.py:66
  51.5 3.4 %collective-permute-start = (bf16[2,512,256]{2,1,0:T(8,128)(2,1)S(1)}, bf16[2,512,256]{2,1,0:T(8,128)(2,1)S(1)}, u32[]{:S(2)}, u32[]{:S(2)}) collective-permute-start(bf16[2,512,256]{2,1,0:T(8,128)(2,1)S(1)} %pad_maximum_fusion.1), channel_id=1, source_target_pairs={{8,0},{12,4},{16,8},{20,12},{24,16},{28,20},{9,1},{13,5},{17,9},{2... | collective-permute-start | bytes 1572872 | tf_op jit(solution)/shard_map/ppermute | solution.py:20
  54.8 2.3 %collective-permute-start.1 = (bf16[2,512,256]{2,1,0:T(8,128)(2,1)S(1)}, bf16[2,512,256]{2,1,0:T(8,128)(2,1)S(1)}, u32[]{:S(2)}, u32[]{:S(2)}) collective-permute-start(bf16[2,512,256]{2,1,0:T(8,128)(2,1)S(1)} %pad_maximum_fusion.1), channel_id=1, source_target_pairs={{4,0},{8,4},{12,8},{16,12},{20,16},{24,20},{28,24},{5,1},{9,5},{13... | collective-permute-start | bytes 1572872 | tf_op jit(solution)/shard_map/ppermute | solution.py:20
  57.1 2.1 %collective-permute-start.2 = (bf16[2,512,256]{2,1,0:T(8,128)(2,1)S(1)}, bf16[2,512,256]{2,1,0:T(8,128)(2,1)S(1)}, u32[]{:S(2)}, u32[]{:S(2)}) collective-permute-start(bf16[2,512,256]{2,1,0:T(8,128)(2,1)S(1)} %pad_maximum_fusion.1), channel_id=1, source_target_pairs={{0,4},{4,8},{8,12},{12,16},{16,20},{20,24},{24,28},{1,5},{5,9},{9,... | collective-permute-start | bytes 1572872 | tf_op jit(solution)/shard_map/ppermute | solution.py:20
  59.2 2.5 %collective-permute-start.3 = (bf16[2,512,256]{2,1,0:T(8,128)(2,1)S(1)}, bf16[2,512,256]{2,1,0:T(8,128)(2,1)S(1)}, u32[]{:S(2)}, u32[]{:S(2)}) collective-permute-start(bf16[2,512,256]{2,1,0:T(8,128)(2,1)S(1)} %pad_maximum_fusion.1), channel_id=1, source_target_pairs={{0,8},{4,12},{8,16},{12,20},{16,24},{20,28},{1,9},{5,13},{9,17},{1... | collective-permute-start | bytes 1572872 | tf_op jit(solution)/shard_map/ppermute | solution.py:20
  61.8 5.4 %collective-permute-done = bf16[2,512,256]{2,1,0:T(8,128)(2,1)S(1)} collective-permute-done((bf16[2,512,256]{2,1,0:T(8,128)(2,1)S(1)}, bf16[2,512,256]{2,1,0:T(8,128)(2,1)S(1)}, u32[]{:S(2)}, u32[]{:S(2)}) %collective-permute-start) | collective-permute-done | bytes 524320 | tf_op jit(solution)/shard_map/ppermute | solution.py:20
  67.2 11.2 %collective-permute-done.1 = bf16[2,512,256]{2,1,0:T(8,128)(2,1)S(1)} collective-permute-done((bf16[2,512,256]{2,1,0:T(8,128)(2,1)S(1)}, bf16[2,512,256]{2,1,0:T(8,128)(2,1)S(1)}, u32[]{:S(2)}, u32[]{:S(2)}) %collective-permute-start.1) | collective-permute-done | bytes 524320 | tf_op jit(solution)/shard_map/ppermute | solution.py:20
  78.4 11.7 %collective-permute-done.3 = bf16[2,512,256]{2,1,0:T(8,128)(2,1)S(1)} collective-permute-done((bf16[2,512,256]{2,1,0:T(8,128)(2,1)S(1)}, bf16[2,512,256]{2,1,0:T(8,128)(2,1)S(1)}, u32[]{:S(2)}, u32[]{:S(2)}) %collective-permute-start.3) | collective-permute-done | bytes 524320 | tf_op jit(solution)/shard_map/ppermute | solution.py:20
  90.6 2.3 %collective-permute-start.4 = (bf16[2,512,256]{2,1,0:T(8,128)(2,1)S(1)}, bf16[2,512,256]{2,1,0:T(8,128)(2,1)S(1)}, u32[]{:S(2)}, u32[]{:S(2)}) collective-permute-start(bf16[2,512,256]{2,1,0:T(8,128)(2,1)S(1)} %add_convert_fusion), channel_id=1, source_target_pairs={{2,0},{3,1},{6,4},{7,5},{10,8},{11,9},{14,12},{15,13},{18,16},{19,... | collective-permute-start | bytes 1572872 | tf_op jit(solution)/shard_map/ppermute | solution.py:20
  92.9 2.6 %collective-permute-start.5 = (bf16[2,512,256]{2,1,0:T(8,128)(2,1)S(1)}, bf16[2,512,256]{2,1,0:T(8,128)(2,1)S(1)}, u32[]{:S(2)}, u32[]{:S(2)}) collective-permute-start(bf16[2,512,256]{2,1,0:T(8,128)(2,1)S(1)} %add_convert_fusion), channel_id=1, source_target_pairs={{1,0},{2,1},{3,2},{5,4},{6,5},{7,6},{9,8},{10,9},{11,10},{13,12},{... | collective-permute-start | bytes 1572872 | tf_op jit(solution)/shard_map/ppermute | solution.py:20
  95.6 1.3 collective-permute-start.6
  96.9 1.3 collective-permute-start.7
  98.2 7.0 %collective-permute-done.4 = bf16[2,512,256]{2,1,0:T(8,128)(2,1)S(1)} collective-permute-done((bf16[2,512,256]{2,1,0:T(8,128)(2,1)S(1)}, bf16[2,512,256]{2,1,0:T(8,128)(2,1)S(1)}, u32[]{:S(2)}, u32[]{:S(2)}) %collective-permute-start.4) | collective-permute-done | bytes 524320 | tf_op jit(solution)/shard_map/ppermute | solution.py:20
  105.2 8.9 %collective-permute-done.5 = bf16[2,512,256]{2,1,0:T(8,128)(2,1)S(1)} collective-permute-done((bf16[2,512,256]{2,1,0:T(8,128)(2,1)S(1)}, bf16[2,512,256]{2,1,0:T(8,128)(2,1)S(1)}, u32[]{:S(2)}, u32[]{:S(2)}) %collective-permute-start.5) | collective-permute-done | bytes 524320 | tf_op jit(solution)/shard_map/ppermute | solution.py:20
  114.1 17.4 %collective-permute-done.7 = bf16[2,512,256]{2,1,0:T(8,128)(2,1)S(1)} collective-permute-done((bf16[2,512,256]{2,1,0:T(8,128)(2,1)S(1)}, bf16[2,512,256]{2,1,0:T(8,128)(2,1)S(1)}, u32[]{:S(2)}, u32[]{:S(2)}) %collective-permute-start.7) | collective-permute-done | bytes 524320 | tf_op jit(solution)/shard_map/ppermute | solution.py:20
  132.1 2.4 %fusion.36 = (bf16[512,256]{1,0:T(8,128)(2,1)S(1)}, bf16[512,256]{1,0:T(8,128)(2,1)S(1)}) fusion(f32[2,512,256]{2,1,0:T(8,128)S(1)} %multiply_add_fusion, f32[256]{0:T(256)S(1)} %fusion.81, f32[512]{0:T(512)S(1)} %fusion.75), kind=kLoop, calls=%fused_computation.56 | loop fusion | flops 1179648 | bytes 1575936 | tf_op jit(solution)/shard_map/convert_element_type | solution.py:172
  138.0 5.0 %fusion.40 = f32[512,256]{1,0:T(8,128)S(1)} fusion(bf16[512,256]{1,0:T(8,128)(2,1)S(1)} %fusion.19), kind=kOutput, calls=%fused_computation.63 | convolution fusion | flops 138149888 | bytes 786432 | tf_op jit(solution)/shard_map/dot_general | solution.py:63
  142.9 1.2 fusion.20
  144.2 5.0 %fusion.39 = f32[512,256]{1,0:T(8,128)S(1)} fusion(bf16[512,256]{1,0:T(8,128)(2,1)S(1)} %fusion.20), kind=kOutput, calls=%fused_computation.62 | convolution fusion | flops 138149888 | bytes 786432 | tf_op jit(solution)/shard_map/dot_general | solution.py:65
  149.2 5.1 %fusion.14 = f32[1,512,256]{2,1,0:T(8,128)S(1)} fusion(f32[512,256]{1,0:T(8,128)S(1)} %fusion.40, bf16[512,256]{1,0:T(8,128)(2,1)S(1)} %fusion.20), kind=kOutput, calls=%fused_computation.25 | convolution fusion | flops 138412032 | bytes 1310720 | tf_op jit(solution)/shard_map/dot_general | solution.py:64
  154.3 5.1 %fusion.12 = f32[1,512,256]{2,1,0:T(8,128)S(1)} fusion(f32[512,256]{1,0:T(8,128)S(1)} %fusion.39, bf16[512,256]{1,0:T(8,128)(2,1)S(1)} %fusion.19), kind=kOutput, calls=%fused_computation.22 | convolution fusion | flops 138412032 | bytes 1310720 | tf_op jit(solution)/shard_map/dot_general | solution.py:66
  (43 shorter events, 18.3 us)
Async XLA Ops:
  4.6 7.8 %all-to-all-start = ((s32[8,24,2]{1,2,0:T(2,128)}), s32[8,24,2]{1,2,0:T(2,128)S(1)}, u32[]{:S(2)}, u32[]{:S(2)}) async-start(s32[8,24,2]{1,2,0:T(2,128)} %copy.17), calls=%async_computation | async-start | bytes 16384 | tf_op jit(solution)/shard_map/all_to_all | solution.py:116
  12.4 9.2 %all-to-all-start.1 = ((bf16[8,24,512]{2,1,0:T(8,128)(2,1)}), bf16[8,24,512]{2,1,0:T(8,128)(2,1)S(1)}, u32[]{:S(2)}, u32[]{:S(2)}) async-start(bf16[8,24,512]{2,1,0:T(8,128)(2,1)} %bitcast.13), calls=%async_computation.1 | async-start | bytes 393216 | tf_op jit(solution)/shard_map/all_to_all | solution.py:109
  51.5 15.7 %collective-permute-start = (bf16[2,512,256]{2,1,0:T(8,128)(2,1)S(1)}, bf16[2,512,256]{2,1,0:T(8,128)(2,1)S(1)}, u32[]{:S(2)}, u32[]{:S(2)}) collective-permute-start(bf16[2,512,256]{2,1,0:T(8,128)(2,1)S(1)} %pad_maximum_fusion.1), channel_id=1, source_target_pairs={{8,0},{12,4},{16,8},{20,12},{24,16},{28,20},{9,1},{13,5},{17,9},{2... | collective-permute-start | bytes 1572872 | tf_op jit(solution)/shard_map/ppermute | solution.py:20
  54.8 23.6 %collective-permute-start.1 = (bf16[2,512,256]{2,1,0:T(8,128)(2,1)S(1)}, bf16[2,512,256]{2,1,0:T(8,128)(2,1)S(1)}, u32[]{:S(2)}, u32[]{:S(2)}) collective-permute-start(bf16[2,512,256]{2,1,0:T(8,128)(2,1)S(1)} %pad_maximum_fusion.1), channel_id=1, source_target_pairs={{4,0},{8,4},{12,8},{16,12},{20,16},{24,20},{28,24},{5,1},{9,5},{13... | collective-permute-start | bytes 1572872 | tf_op jit(solution)/shard_map/ppermute | solution.py:20
  57.1 21.3 %collective-permute-start.2 = (bf16[2,512,256]{2,1,0:T(8,128)(2,1)S(1)}, bf16[2,512,256]{2,1,0:T(8,128)(2,1)S(1)}, u32[]{:S(2)}, u32[]{:S(2)}) collective-permute-start(bf16[2,512,256]{2,1,0:T(8,128)(2,1)S(1)} %pad_maximum_fusion.1), channel_id=1, source_target_pairs={{0,4},{4,8},{8,12},{12,16},{16,20},{20,24},{24,28},{1,5},{5,9},{9,... | collective-permute-start | bytes 1572872 | tf_op jit(solution)/shard_map/ppermute | solution.py:20
  59.2 30.9 %collective-permute-start.3 = (bf16[2,512,256]{2,1,0:T(8,128)(2,1)S(1)}, bf16[2,512,256]{2,1,0:T(8,128)(2,1)S(1)}, u32[]{:S(2)}, u32[]{:S(2)}) collective-permute-start(bf16[2,512,256]{2,1,0:T(8,128)(2,1)S(1)} %pad_maximum_fusion.1), channel_id=1, source_target_pairs={{0,8},{4,12},{8,16},{12,20},{16,24},{20,28},{1,9},{5,13},{9,17},{1... | collective-permute-start | bytes 1572872 | tf_op jit(solution)/shard_map/ppermute | solution.py:20
  90.6 14.6 %collective-permute-start.4 = (bf16[2,512,256]{2,1,0:T(8,128)(2,1)S(1)}, bf16[2,512,256]{2,1,0:T(8,128)(2,1)S(1)}, u32[]{:S(2)}, u32[]{:S(2)}) collective-permute-start(bf16[2,512,256]{2,1,0:T(8,128)(2,1)S(1)} %add_convert_fusion), channel_id=1, source_target_pairs={{2,0},{3,1},{6,4},{7,5},{10,8},{11,9},{14,12},{15,13},{18,16},{19,... | collective-permute-start | bytes 1572872 | tf_op jit(solution)/shard_map/ppermute | solution.py:20
  92.9 21.2 %collective-permute-start.5 = (bf16[2,512,256]{2,1,0:T(8,128)(2,1)S(1)}, bf16[2,512,256]{2,1,0:T(8,128)(2,1)S(1)}, u32[]{:S(2)}, u32[]{:S(2)}) collective-permute-start(bf16[2,512,256]{2,1,0:T(8,128)(2,1)S(1)} %add_convert_fusion), channel_id=1, source_target_pairs={{1,0},{2,1},{3,2},{5,4},{6,5},{7,6},{9,8},{10,9},{11,10},{13,12},{... | collective-permute-start | bytes 1572872 | tf_op jit(solution)/shard_map/ppermute | solution.py:20
  95.6 18.6 %collective-permute-start.6 = (bf16[2,512,256]{2,1,0:T(8,128)(2,1)S(1)}, bf16[2,512,256]{2,1,0:T(8,128)(2,1)S(1)}, u32[]{:S(2)}, u32[]{:S(2)}) collective-permute-start(bf16[2,512,256]{2,1,0:T(8,128)(2,1)S(1)} %add_convert_fusion), channel_id=1, source_target_pairs={{0,1},{1,2},{2,3},{4,5},{5,6},{6,7},{8,9},{9,10},{10,11},{12,13},{... | collective-permute-start | bytes 1572872 | tf_op jit(solution)/shard_map/ppermute | solution.py:20
  96.9 34.7 %collective-permute-start.7 = (bf16[2,512,256]{2,1,0:T(8,128)(2,1)S(1)}, bf16[2,512,256]{2,1,0:T(8,128)(2,1)S(1)}, u32[]{:S(2)}, u32[]{:S(2)}) collective-permute-start(bf16[2,512,256]{2,1,0:T(8,128)(2,1)S(1)} %add_convert_fusion), channel_id=1, source_target_pairs={{0,2},{1,3},{4,6},{5,7},{8,10},{9,11},{12,14},{13,15},{16,18},{17,... | collective-permute-start | bytes 1572872 | tf_op jit(solution)/shard_map/ppermute | solution.py:20
where the time goes:
time: 161 us
  waiting for transfers between devices  66 us (41%)
  matrix products  49.5 us (31%)
  starting transfers between devices  26.4 us (16%)
  other arithmetic  10.4 us (6%)
  local copies, waits for them, and re-layouts  7.9 us (5%)
    ppermute x8, waiting for transfers between devices, from_behind(): lax.ppermute(value, axis, [(source, source + steps) for source in range(l...  61.6 us
    ppermute x8, starting transfers between devices, from_behind(): lax.ppermute(value, axis, [(source, source + steps) for source in range(l...  17.7 us
    dot_general x2, matrix products, left_apply(): imag_imag = jnp.dot(table_i, imag_part, preferred_element_type=jnp.float32)  9.29 us
    dot_general x2, matrix products, left_apply(): imag_real = jnp.dot(table_i, real_part, preferred_element_type=jnp.float32)  9.28 us
    dot_general x2, matrix products, left_apply(): real_real = jnp.dot(table_r, real_part, preferred_element_type=jnp.float32)  9.2 us
    dot_general x2, matrix products, left_apply(): real_imag = jnp.dot(table_r, imag_part, preferred_element_type=jnp.float32)  8.98 us
    all_to_all x1, starting transfers between devices, local(): lax.all_to_all(outgoing.reshape(wide_count, slot_count, 2 * FACET * FACET...  4.45 us
    all_to_all x1, waiting for transfers between devices, local(): lax.all_to_all(outgoing.reshape(wide_count, slot_count, 2 * FACET * FACET...  4.37 us
  transfers between devices with their start and end apart: 10, of which 7 were waited for; matrix products, arithmetic and copies ran while one was open for 3% of the time, Pallas kernels for 0%

commit v1 on v0

v1 whole, which is shorter than its diff:
```python
import math

import jax
import jax.numpy as jnp
import numpy as np
from jax import lax
from jax.sharding import PartitionSpec as P

TH = 512
TW = 256
FACET = 16
DEPTH = 1280
REACH = 2
SPREAD = 16.0
PIXELS = FACET * FACET
WORDS = 2 * PIXELS + 128


def dft_tables(length, spin_sign):
    position = np.arange(length)
    angles = (position[:, None] * position[None, :] % length) * (2.0 * math.pi / length)
    as_bf16 = lambda v: np.asarray(v, np.float32).astype(jnp.bfloat16)
    return as_bf16(np.cos(angles)), as_bf16(spin_sign * np.sin(angles))


def signed_frequency(length):
    return (np.arange(length) + length // 2) % length - length // 2


def reach_weight(length, offset):
    travel = signed_frequency(length) * (DEPTH / (length * length))
    return np.exp(-((travel - offset) ** 2) / SPREAD).astype(np.float32)


def depth_phase(length):
    frequency = signed_frequency(length)
    return (DEPTH * frequency * frequency % (2 * length * length)) * (-math.pi / (length * length))


def render(amplitude, tilt):
    position = jnp.arange(PIXELS, dtype=jnp.int32)
    row_pos = (position // FACET).astype(jnp.float32)
    col_pos = (position % FACET).astype(jnp.float32)
    phase = (
        tilt[0][:, None] * row_pos[None, :] + tilt[1][:, None] * col_pos[None, :] + tilt[2][:, None]
    )
    return (
        (amplitude * jnp.cos(phase)).astype(jnp.bfloat16),
        (amplitude * jnp.sin(phase)).astype(jnp.bfloat16),
    )


def dot(a, b):
    return jnp.dot(a, b, preferred_element_type=jnp.float32)


def left_apply(table, pair):
    both = dot(table, pair)
    half, wide = table.shape[0] // 2, pair.shape[1] // 2
    top, low = both[:half], both[half:]
    return top[:, :wide] - low[:, wide:], top[:, wide:] + low[:, :wide]


def right_apply(pair, table):
    both = dot(pair, table)
    half, wide = pair.shape[0] // 2, table.shape[1] // 2
    top, low = both[:half], both[half:]
    return top[:, :wide] - low[:, wide:], top[:, wide:] + low[:, :wide]


def exchange(amplitude, tilt, owner, row_offset, col_offset):
    wide_count, narrow_count = lax.axis_size("wide"), lax.axis_size("narrow")
    band = lax.axis_index("narrow")
    facet_count = amplitude.shape[0]
    slot_count = max(2, (3 * facet_count + wide_count - 1) // wide_count)
    total_slots = wide_count * slot_count
    field_r, field_i = render(amplitude, tilt)
    marks = jnp.stack(
        [owner[:, 0], row_offset // 16, row_offset % 16, col_offset // 16, col_offset % 16], axis=1
    ).astype(jnp.bfloat16)
    marks = jnp.pad(marks, ((0, 0), (0, 128 - marks.shape[1])))
    packed = jnp.concatenate([field_r, field_i, marks], axis=1)
    packed = lax.all_gather(packed, "narrow", axis=0, tiled=False)
    bands = min(narrow_count, 2 * REACH + 1)
    first = jnp.clip(band - REACH, 0, narrow_count - bands)
    if bands < narrow_count:
        packed = lax.dynamic_slice_in_dim(packed, first, bands, 0)
    target = packed[:, :, 2 * PIXELS].astype(jnp.int32)
    chosen = target[:, :, None] == jnp.arange(wide_count, dtype=jnp.int32)[None, None, :]
    earlier = jnp.asarray(np.tril(np.ones((facet_count, facet_count), np.float32), -1), jnp.bfloat16)
    rank = jnp.einsum(
        "fg,bgc->bfc", earlier, chosen.astype(jnp.bfloat16), preferred_element_type=jnp.float32
    )
    rank = jnp.sum(jnp.where(chosen, rank, 0.0), axis=2).astype(jnp.int32)
    slot_at = target * slot_count + rank
    pick = slot_at[:, None, :] == jnp.arange(total_slots, dtype=jnp.int32)[None, :, None]
    outgoing = jnp.einsum(
        "bsf,bfp->bsp", pick.astype(jnp.bfloat16), packed, preferred_element_type=jnp.float32
    ).astype(jnp.bfloat16)
    incoming = lax.all_to_all(
        outgoing.reshape(bands, wide_count, slot_count, WORDS),
        "wide",
        split_axis=1,
        concat_axis=1,
        tiled=True,
    )
    return incoming.reshape(bands, total_slots, WORDS), band - first


def place(incoming):
    bands, total_slots, _ = incoming.shape
    fields = incoming[:, :, : 2 * PIXELS].reshape(bands, total_slots, 2, FACET, FACET)
    marks = incoming[:, :, 2 * PIXELS : 2 * PIXELS + 8].astype(jnp.int32)
    row_at = marks[:, :, 1] * 16 + marks[:, :, 2]
    col_at = marks[:, :, 3] * 16 + marks[:, :, 4]
    pixel = jnp.arange(FACET, dtype=jnp.int32)
    col_hot = (
        jnp.arange(TW, dtype=jnp.int32) == col_at[:, :, None, None] + pixel[:, None]
    ).astype(jnp.bfloat16)
    spread = jnp.einsum(
        "bscuv,bsvx->bsucx", fields, col_hot, preferred_element_type=jnp.float32
    ).astype(jnp.bfloat16)
    row_hot = (
        jnp.arange(TH, dtype=jnp.int32)[:, None, None] == row_at[:, None, :, None] + pixel
    ).astype(jnp.bfloat16)
    plane = jnp.einsum(
        "byk,bkx->byx",
        row_hot.reshape(bands, TH, total_slots * FACET),
        spread.reshape(bands, total_slots * FACET, 2 * TW),
        preferred_element_type=jnp.float32,
    )
    return plane.astype(jnp.bfloat16)


def local(amplitude, tilt, owner, row_offset, col_offset):
    wide_count = lax.axis_size("wide")
    column = lax.axis_index("wide")
    incoming, here = exchange(amplitude, tilt, owner, row_offset, col_offset)
    plane = place(incoming)
    bands = plane.shape[0]
    scale = 1.0 / math.sqrt(TH * TW)

    most = bands - 1
    by_offset = np.zeros((2 * most + 1, TH), np.float32)
    for offset in range(-REACH, REACH + 1):
        if abs(offset) <= most:
            by_offset[offset + most] = reach_weight(TH, float(offset))
    weights = lax.dynamic_slice_in_dim(jnp.asarray(by_offset[::-1].copy()), most - here, bands, 0)
    fwd_hr, fwd_hi = dft_tables(TH, -1.0)
    fwd_h = jnp.asarray(np.concatenate([fwd_hr, fwd_hi], axis=0))
    row_w = jnp.concatenate([weights, weights], axis=1)
    tables = (row_w[:, :, None] * fwd_h[None].astype(jnp.float32)).astype(jnp.bfloat16)
    tables = jnp.transpose(tables, (1, 0, 2)).reshape(2 * TH, bands * TH)
    rows_r, rows_i = left_apply(tables, plane.reshape(bands * TH, 2 * TW))
    fwd_w = jnp.asarray(np.concatenate(dft_tables(TW, -1.0), axis=1))
    pair = jnp.concatenate([rows_r, rows_i], axis=0).astype(jnp.bfloat16)
    spec_r, spec_i = right_apply(pair, fwd_w)
    spectrum = (jnp.stack([spec_r, spec_i]) * scale).astype(jnp.bfloat16)

    rows = TH // wide_count
    parts = lax.all_to_all(
        spectrum.reshape(2, wide_count, rows, TW), "wide", split_axis=1, concat_axis=1, tiled=True
    )
    padded = jnp.pad(parts.astype(jnp.float32), ((0, 0), (REACH, REACH), (0, 0), (0, 0)))
    total = 0.0
    for offset in range(-REACH, REACH + 1):
        start = REACH - offset
        total = total + jnp.asarray(reach_weight(TW, float(offset))) * padded[
            :, start : start + wide_count
        ]
    angle = depth_phase(TH)[:, None] + depth_phase(TW)[None, :]
    phase_r = lax.dynamic_slice_in_dim(
        jnp.asarray(np.cos(angle).astype(np.float32)), column * rows, rows, 0
    )
    phase_i = lax.dynamic_slice_in_dim(
        jnp.asarray(np.sin(angle).astype(np.float32)), column * rows, rows, 0
    )
    focus = jnp.stack(
        [phase_r * total[0] - phase_i * total[1], phase_r * total[1] + phase_i * total[0]]
    ).astype(jnp.bfloat16)
    focus = lax.all_to_all(focus, "wide", split_axis=1, concat_axis=1, tiled=True)
    inv_w = jnp.asarray(np.concatenate(dft_tables(TW, 1.0), axis=1))
    inv_h = jnp.asarray(np.concatenate(dft_tables(TH, 1.0), axis=0))
    cols_r, cols_i = right_apply(focus.reshape(2 * TH, TW), inv_w)
    pair = jnp.concatenate([cols_r, cols_i], axis=1).astype(jnp.bfloat16)
    out_r, out_i = left_apply(inv_h, pair)
    return jnp.stack([out_r, out_i]) * scale


def solution(mesh):
    in_specs = (
        P(("wide", "narrow"), None),
        P(None, ("wide", "narrow")),
        P(("wide", "narrow"), None),
        P(("wide", "narrow")),
        P(("wide", "narrow")),
    )
    out_specs = P(None, "narrow", "wide")
    return jax.shard_map(local, mesh=mesh, in_specs=in_specs, out_specs=out_specs, check_vma=False)
```

time: 161 us -> 133 us (0.83)
  the two profiles are of different devices: /device:TPU:28 before, /device:TPU:0 now
where the time goes in v1:
time: 133 us; the launch traced here: 132 us
  local copies, waits for them, and re-layouts  42.9 us (32%)
  blocking collectives  28.1 us (21%)
  waiting for transfers between devices  23.3 us (18%)
  matrix products  23 us (17%)
  starting transfers between devices  7.22 us (5%)
  other arithmetic  6.91 us (5%)
    reshape x1, local copies, waits for them, and re-layouts, place(): spread.reshape(bands, total_slots * FACET, 2 * TW)  20.5 us
    all_gather x1, blocking collectives, exchange(): packed = lax.all_gather(packed, 'narrow', axis=0, tiled=False)  15.8 us
    dot_general x4, matrix products, dot(): return jnp.dot(a, b, preferred_element_type=jnp.float32)  15.7 us
    all_to_all x1, waiting for transfers between devices, exchange(): lax.all_to_all(outgoing.reshape(bands, wide_count, slot_count, WORDS), 'w...  14.6 us
    all_to_all x1, blocking collectives, local(): lax.all_to_all(focus, 'wide', split_axis=1, concat_axis=1, tiled=True)  12.3 us
    convert_element_type x1, local copies, waits for them, and re-layouts, place(): spread = jnp.einsum('bscuv,bsvx->bsucx', fields, col_hot, preferred_eleme...  11.5 us
    all_to_all x1, waiting for transfers between devices, local(): lax.all_to_all(spectrum.reshape(2, wide_count, rows, TW), 'wide', split_a...  8.77 us
    reshape x1, local copies, waits for them, and re-layouts, place(): incoming[:, :, :2 * PIXELS].reshape(bands, total_slots, 2, FACET, FACET)  6.71 us
  transfers between devices with their start and end apart: 2, of which 2 were waited for; matrix products, arithmetic and copies ran while one was open for 1% of the time, Pallas kernels for 0%

profile of v1, /device:TPU:0, one launch (start us, length us, event | category | flops | bytes accessed | tf_op | source)
XLA Modules:
  0.0 131.8 jit_solution(4575010918857199769)
XLA Ops:
  0.0 0.7 convert.38
  0.7 0.7 fusion.52
  1.5 0.8 slice_bitcast_fusion.2
  2.3 1.2 multiply_convert_fusion.5
  3.5 15.8 %all-gather = bf16[256,640]{1,0:T(8,128)(2,1)S(1)} all-gather(bf16[64,640]{1,0:T(8,128)(2,1)S(1)} %fusion.45), channel_id=2, replica_groups=mesh['wide'=8,'narrow'=4] {'narrow'}, dimensions={0}, use_global_device_ids=true | all-gather | bytes 409600 | tf_op jit(solution)/shard_map/all_gather | solution.py:83
  19.3 0.2 convert_reduce_fusion
  19.6 0.9 fusion.16
  20.5 0.6 convolution_convert_fusion
  21.0 1.0 copy.37
  22.1 3.7 %all-to-all-start = ((bf16[4,8,24,640]{3,2,0,1:T(8,128)(2,1)}), bf16[4,8,24,640]{3,2,0,1:T(8,128)(2,1)S(1)}, u32[]{:S(2)}, u32[]{:S(2)}) async-start(bf16[4,8,24,640]{3,2,0,1:T(8,128)(2,1)} %copy.37), calls=%async_computation | async-start | bytes 1966080 | tf_op jit(solution)/shard_map/all_to_all | solution.py:100
  26.0 14.6 %all-to-all-done = bf16[4,8,24,640]{3,2,0,1:T(8,128)(2,1)S(1)} async-done(((bf16[4,8,24,640]{3,2,0,1:T(8,128)(2,1)}), bf16[4,8,24,640]{3,2,0,1:T(8,128)(2,1)S(1)}, u32[]{:S(2)}, u32[]{:S(2)}) %all-to-all-start) | async-done | bytes 983072 | tf_op jit(solution)/shard_map/all_to_all | solution.py:100
  40.7 0.8 fusion.41
  41.5 0.2 iota_add_fusion
  41.7 0.5 copy.39
  42.2 6.7 %copy.40 = bf16[4,192,2,16,16]{4,3,2,1,0:T(8,128)(2,1)} copy(bf16[4,192,2,16,16]{1,4,3,2,0:T(8,128)(2,1)S(1)} %bitcast.57) | data formatting | bytes 1572864 | tf_op jit(solution)/shard_map/reshape | solution.py:112
  48.9 5.8 %convert_bitcast_fusion = bf16[4,192,16,2,256]{4,2,3,1,0:T(8,128)(2,1)S(1)} fusion(bf16[4,192,2,16,16]{4,3,2,1,0:T(8,128)(2,1)} %copy.40, s32[4,192,16]{2,1,0:T(8,128)S(1)} %iota_add_fusion), kind=kOutput, calls=%fused_computation.2 | convolution fusion | flops 210763776 | bytes 13418496 | tf_op jit(solution)/shard_map/bscuv,bsvx->bsucx/dot_general | solution.py:120
  54.8 11.5 %copy.41 = bf16[4,192,16,2,256]{4,3,2,1,0:T(2,128)(2,1)} copy(bf16[4,192,16,2,256]{4,2,3,1,0:T(8,128)(2,1)S(1)} %convert_bitcast_fusion) | data formatting | bytes 25165824 | tf_op jit(solution)/shard_map/convert_element_type | solution.py:122
  66.3 20.5 %reshape.119 = bf16[4,3072,512]{2,1,0:T(8,128)(2,1)} reshape(bf16[4,192,16,2,256]{4,3,2,1,0:T(2,128)(2,1)} %copy.41) | data formatting | bytes 25165824 | tf_op jit(solution)/shard_map/reshape | solution.py:129
  87.0 0.2 add.163
  87.2 14.1 %fusion.12 = f32[1024,512]{1,0:T(8,128)S(1)} fusion(bf16[4,3072,512]{2,1,0:T(8,128)(2,1)} %reshape.119, s32[4,3072]{1,0:T(4,128)S(1)} %broadcast_add_fusion, f32[1024,512]{1,0:T(8,128)} %constant.135, f32[1024,4]{0,1:T(4,128)S(1)} %maximum_bitcast_fusion), kind=kOutput, calls=%fused_computation.17 | convolution fusion | flops 8601468928 | bytes 16842752 | tf_op jit(solution)/shard_map/dot_general | solution.py:54
  101.4 0.4 fusion.32
  102.1 0.9 fusion.25
  103.0 3.5 %all-to-all-start.1 = ((bf16[2,8,64,256]{3,2,0,1:T(8,128)(2,1)}), bf16[2,8,64,256]{3,2,0,1:T(8,128)(2,1)S(1)}, u32[]{:S(2)}, u32[]{:S(2)}) async-start(bf16[2,8,64,256]{3,2,0,1:T(8,128)(2,1)} %fusion.25), calls=%async_computation.1 | async-start | bytes 1048576 | tf_op jit(solution)/shard_map/all_to_all | solution.py:161
  106.5 0.9 constant_dynamic-slice_fusion
  107.4 8.8 %all-to-all-done.1 = bf16[2,8,64,256]{3,2,0,1:T(8,128)(2,1)S(1)} async-done(((bf16[2,8,64,256]{3,2,0,1:T(8,128)(2,1)}), bf16[2,8,64,256]{3,2,0,1:T(8,128)(2,1)S(1)}, u32[]{:S(2)}, u32[]{:S(2)}) %all-to-all-start.1) | async-done | bytes 524320 | tf_op jit(solution)/shard_map/all_to_all | solution.py:161
  116.3 0.3 fusion.21
  116.6 0.2 subtract_convert_fusion
  116.8 12.3 %all_to_all.15 = bf16[2,8,64,256]{3,2,0,1:T(8,128)(2,1)S(1)} all-to-all(bf16[2,8,64,256]{3,2,0,1:T(8,128)(2,1)S(1)} %pad_maximum_fusion), channel_id=1, replica_groups=mesh['wide'=8,'narrow'=4] {'wide'}, dimensions={1} | all-to-all | bytes 1048576 | tf_op jit(solution)/shard_map/all_to_all | solution.py:181
  129.2 0.5 fusion.57
  129.7 0.2 fusion.29
  129.8 0.7 fusion.36
  130.7 1.1 maximum_multiply_fusion.1
  (38 shorter events, 1.3 us)
Async XLA Ops:
  0.0 25.9 %copy-start.3 = (f32[7,512]{1,0:T(8,128)S(1)}, f32[7,512]{1,0:T(8,128)}, u32[]{:S(2)}) copy-start(f32[7,512]{1,0:T(8,128)} %constant.119.clone) | copy-start | bytes 43012
  22.1 18.4 %all-to-all-start = ((bf16[4,8,24,640]{3,2,0,1:T(8,128)(2,1)}), bf16[4,8,24,640]{3,2,0,1:T(8,128)(2,1)S(1)}, u32[]{:S(2)}, u32[]{:S(2)}) async-start(bf16[4,8,24,640]{3,2,0,1:T(8,128)(2,1)} %copy.37), calls=%async_computation | async-start | bytes 1966080 | tf_op jit(solution)/shard_map/all_to_all | solution.py:100
  87.2 14.2 %copy-start.2 = (bf16[256,512]{1,0:T(8,128)(2,1)S(1)}, bf16[256,512]{1,0:T(8,128)(2,1)}, u32[]{:S(2)}) copy-start(bf16[256,512]{1,0:T(8,128)(2,1)} %constant.121.clone) | copy-start | bytes 786436
  101.8 14.4 %copy-start.4 = (f32[256]{0:T(256)S(1)}, f32[256]{0:T(256)}, u32[]{:S(2)}) copy-start(f32[256]{0:T(256)} %constant.122.clone) | copy-start | bytes 3076
  101.9 14.4 %copy-start.5 = (f32[256]{0:T(256)S(1)}, f32[256]{0:T(256)}, u32[]{:S(2)}) copy-start(f32[256]{0:T(256)} %constant.123.clone) | copy-start | bytes 3076
  101.9 14.4 %copy-start.6 = (f32[256]{0:T(256)S(1)}, f32[256]{0:T(256)}, u32[]{:S(2)}) copy-start(f32[256]{0:T(256)} %constant.124.clone) | copy-start | bytes 3076
  101.9 14.4 %copy-start.7 = (f32[256]{0:T(256)S(1)}, f32[256]{0:T(256)}, u32[]{:S(2)}) copy-start(f32[256]{0:T(256)} %constant.125.clone) | copy-start | bytes 3076
  101.9 14.4 %copy-start.8 = (f32[256]{0:T(256)S(1)}, f32[256]{0:T(256)}, u32[]{:S(2)}) copy-start(f32[256]{0:T(256)} %constant.126.clone) | copy-start | bytes 3076
  103.0 13.2 %all-to-all-start.1 = ((bf16[2,8,64,256]{3,2,0,1:T(8,128)(2,1)}), bf16[2,8,64,256]{3,2,0,1:T(8,128)(2,1)S(1)}, u32[]{:S(2)}, u32[]{:S(2)}) async-start(bf16[2,8,64,256]{3,2,0,1:T(8,128)(2,1)} %fusion.25), calls=%async_computation.1 | async-start | bytes 1048576 | tf_op jit(solution)/shard_map/all_to_all | solution.py:161
  107.4 21.8 %copy-start.1 = (bf16[256,512]{1,0:T(8,128)(2,1)S(1)}, bf16[256,512]{1,0:T(8,128)(2,1)}, u32[]{:S(2)}) copy-start(bf16[256,512]{1,0:T(8,128)(2,1)} %constant.129.clone) | copy-start | bytes 786436
  116.8 13.1 %copy-start = (bf16[1024,512]{1,0:T(8,128)(2,1)S(1)}, bf16[1024,512]{1,0:T(8,128)(2,1)}, u32[]{:S(2)}) copy-start(bf16[1024,512]{1,0:T(8,128)(2,1)} %constant.130.clone) | copy-start | bytes 3145732

commit v2 on v1

--- a/solution.py
+++ b/solution.py
@@ -1,9 +1,12 @@
+import functools
 import math
 
 import jax
 import jax.numpy as jnp
 import numpy as np
 from jax import lax
+from jax.experimental import pallas as pl
+from jax.experimental.pallas import tpu as pltpu
 from jax.sharding import PartitionSpec as P
 
 TH = 512
@@ -37,17 +40,47 @@
     return (DEPTH * frequency * frequency % (2 * length * length)) * (-math.pi / (length * length))
 
 
-def render(amplitude, tilt):
-    position = jnp.arange(PIXELS, dtype=jnp.int32)
-    row_pos = (position // FACET).astype(jnp.float32)
-    col_pos = (position % FACET).astype(jnp.float32)
-    phase = (
-        tilt[0][:, None] * row_pos[None, :] + tilt[1][:, None] * col_pos[None, :] + tilt[2][:, None]
-    )
-    return (
-        (amplitude * jnp.cos(phase)).astype(jnp.bfloat16),
-        (amplitude * jnp.sin(phase)).astype(jnp.bfloat16),
-    )
+def render_kernel(amp_ref, par_ref, out_ref):
+    par = par_ref[...]
+    tilt_r, tilt_c, lead = par[:, 0:1], par[:, 1:2], par[:, 2:3]
+    owner, row_at, col_at = par[:, 3:4], par[:, 4:5], par[:, 5:6]
+    lane = lax.broadcasted_iota(jnp.int32, amp_ref.shape, 1)
+    across = lane % FACET
+    col_hi = jnp.floor(col_at * (1.0 / FACET))
+    col_lo = col_at - FACET * col_hi
+    row_hi = jnp.floor(row_at * (1.0 / FACET))
+    row_lo = row_at - FACET * row_hi
+    turn = col_lo.astype(jnp.int32)
+    amp = amp_ref[...]
+    for step in (1, 2, 4, 8):
+        near = pltpu.roll(amp, step, 1)
+        far = pltpu.roll(amp, PIXELS + step - FACET, 1)
+        turned = jnp.where(across >= step, near, far)
+        amp = jnp.where((turn & step) != 0, turned, amp)
+    pixel = ((across - turn) & (FACET - 1)).astype(jnp.float32)
+    phase = tilt_r * (lane // FACET).astype(jnp.float32) + tilt_c * pixel + lead
+    real, imag = (amp * jnp.cos(phase)).astype(jnp.bfloat16), (amp * jnp.sin(phase)).astype(jnp.bfloat16)
+    half = PIXELS // 2
+    out_ref[:, 0:half] = real[:, :half]
+    out_ref[:, half : 2 * half] = imag[:, :half]
+    out_ref[:, 2 * half : 3 * half] = real[:, half:]
+    out_ref[:, 3 * half : 4 * half] = imag[:, half:]
+    spot = lax.broadcasted_iota(jnp.int32, (amp.shape[0], 128), 1)
+    marks = jnp.where(spot == 0, owner, 0.0)
+    for at, value in ((1, row_hi), (2, row_lo), (3, col_hi), (4, col_lo)):
+        marks = jnp.where(spot == at, value, marks)
+    out_ref[:, 4 * half :] = marks.astype(jnp.bfloat16)
+
+
+def render(amplitude, tilt, owner, row_offset, col_offset):
+    par = jnp.concatenate(
+        [tilt, jnp.stack([owner[:, 0], row_offset, col_offset]).astype(jnp.float32)], axis=0
+    )
+    par = jnp.pad(par.T, ((0, 0), (0, 2)))
+    return pl.pallas_call(
+        render_kernel,
+        out_shape=jax.ShapeDtypeStruct((amplitude.shape[0], WORDS), jnp.bfloat16),
+    )(amplitude, par)
 
 
 def dot(a, b):
@@ -74,12 +107,7 @@
     facet_count = amplitude.shape[0]
     slot_count = max(2, (3 * facet_count + wide_count - 1) // wide_count)
     total_slots = wide_count * slot_count
-    field_r, field_i = render(amplitude, tilt)
-    marks = jnp.stack(
-        [owner[:, 0], row_offset // 16, row_offset % 16, col_offset // 16, col_offset % 16], axis=1
-    ).astype(jnp.bfloat16)
-    marks = jnp.pad(marks, ((0, 0), (0, 128 - marks.shape[1])))
-    packed = jnp.concatenate([field_r, field_i, marks], axis=1)
+    packed = render(amplitude, tilt, owner, row_offset, col_offset)
     packed = lax.all_gather(packed, "narrow", axis=0, tiled=False)
     bands = min(narrow_count, 2 * REACH + 1)
     first = jnp.clip(band - REACH, 0, narrow_count - bands)
@@ -107,37 +135,82 @@
     return incoming.reshape(bands, total_slots, WORDS), band - first
 
 
-def place(incoming):
-    bands, total_slots, _ = incoming.shape
-    fields = incoming[:, :, : 2 * PIXELS].reshape(bands, total_slots, 2, FACET, FACET)
-    marks = incoming[:, :, 2 * PIXELS : 2 * PIXELS + 8].astype(jnp.int32)
-    row_at = marks[:, :, 1] * 16 + marks[:, :, 2]
-    col_at = marks[:, :, 3] * 16 + marks[:, :, 4]
-    pixel = jnp.arange(FACET, dtype=jnp.int32)
-    col_hot = (
-        jnp.arange(TW, dtype=jnp.int32) == col_at[:, :, None, None] + pixel[:, None]
-    ).astype(jnp.bfloat16)
-    spread = jnp.einsum(
-        "bscuv,bsvx->bsucx", fields, col_hot, preferred_element_type=jnp.float32
-    ).astype(jnp.bfloat16)
-    row_hot = (
-        jnp.arange(TH, dtype=jnp.int32)[:, None, None] == row_at[:, None, :, None] + pixel
-    ).astype(jnp.bfloat16)
-    plane = jnp.einsum(
-        "byk,bkx->byx",
-        row_hot.reshape(bands, TH, total_slots * FACET),
-        spread.reshape(bands, total_slots * FACET, 2 * TW),
-        preferred_element_type=jnp.float32,
-    )
-    return plane.astype(jnp.bfloat16)
+def forward_kernel(bands, slots, pay_ref, tile_ref, tab_ref, wide_ref, out_ref, mask, spread, plane, total):
+    half = PIXELS
+    marks = pay_ref[:, 2 * PIXELS :].astype(jnp.float32)
+    col_at = FACET * marks[:, 3:4] + marks[:, 4:5]
+    spot = (lax.broadcasted_iota(jnp.int32, mask.shape, 1) % TW).astype(jnp.float32) - col_at
+    mask[...] = jnp.where((spot >= 0.0) & (spot < FACET), 1.0, 0.0)
+    for side in range(2):
+        fields = pay_ref[:, side * half : (side + 1) * half]
+
+        def widen(at, _):
+            pixels = dot(fields, tile_ref[at]) * mask[...]
+            pixels = pixels.astype(jnp.bfloat16)
+            row = pl.multiple_of((side * (FACET // 2) + at) * slots, slots)
+            for b in range(bands):
+                spread[b, pl.ds(row, slots), :] = pixels[b * slots : (b + 1) * slots]
+            return 0
+
+        lax.fori_loop(0, FACET // 2, widen, 0)
+    lane = lax.broadcasted_iota(jnp.int32, (8, 128), 1)
+    select = jnp.where(lane == 1, float(FACET), jnp.where(lane == 2, 1.0, 0.0)).astype(jnp.bfloat16)
+    group = 4
+    depth = group * slots
+    spot = lax.broadcasted_iota(jnp.int32, (TH, depth), 0).astype(jnp.float32)
+    for b in range(bands):
+        corner = pay_ref[b * slots : (b + 1) * slots, 2 * PIXELS :]
+        row_at = lax.dot_general(
+            select, corner, (((1,), (1,)), ((), ())), preferred_element_type=jnp.float32
+        )[0:1]
+        row_at = jnp.concatenate([row_at + float(u) for u in range(group)], axis=1)
+        plane[...] = jnp.zeros_like(plane)
+
+        def add_rows(at, _):
+            step = (at * group).astype(jnp.float32)
+            hot = jnp.where(spot == row_at + step, 1.0, 0.0).astype(jnp.bfloat16)
+            plane[...] += dot(hot, spread[b, pl.ds(pl.multiple_of(at * depth, depth), depth), :])
+            return 0
+
+        lax.fori_loop(0, FACET // group, add_rows, 0)
+        rows = dot(tab_ref[:, b * TH : (b + 1) * TH], plane[...].astype(jnp.bfloat16))
+        total[...] = rows if b == 0 else total[...] + rows
+    scale = 1.0 / math.sqrt(TH * TW)
+    real = (total[:TH, :TW] - total[TH:, TW:]).astype(jnp.bfloat16)
+    imag = (total[:TH, TW:] + total[TH:, :TW]).astype(jnp.bfloat16)
+    by_real, by_imag = dot(real, wide_ref[...]), dot(imag, wide_ref[...])
+    out_ref[0] = ((by_real[:, :TW] - by_imag[:, TW:]) * scale).astype(jnp.bfloat16)
+    out_ref[1] = ((by_real[:, TW:] + by_imag[:, :TW]) * scale).astype(jnp.bfloat16)
+
+
+def tile_tables():
+    lane = np.arange(PIXELS)[None, :, None]
+    spot = np.arange(2 * TW)[None, None, :]
+    at = np.arange(FACET // 2)[:, None, None]
+    same = (lane // 128 == spot // TW) & (lane % 128 == at * FACET + spot % FACET)
+    return same.astype(np.float32).astype(jnp.bfloat16)
+
+
+def forward(incoming, tables, fwd_w):
+    bands, slots, _ = incoming.shape
+    return pl.pallas_call(
+        functools.partial(forward_kernel, bands, slots),
+        out_shape=jax.ShapeDtypeStruct((2, TH, TW), jnp.bfloat16),
+        scratch_shapes=[
+            pltpu.VMEM((bands * slots, 2 * TW), jnp.float32),
+            pltpu.VMEM((bands, FACET * slots, 2 * TW), jnp.bfloat16),
+            pltpu.VMEM((TH, 2 * TW), jnp.float32),
+            pltpu.VMEM((2 * TH, 2 * TW), jnp.float32),
+        ],
+        compiler_params=pltpu.CompilerParams(vmem_limit_bytes=48 * 2**20),
+    )(incoming.reshape(bands * slots, WORDS), jnp.asarray(tile_tables()), tables, fwd_w)
 
 
 def local(amplitude, tilt, owner, row_offset, col_offset):
     wide_count = lax.axis_size("wide")
     column = lax.axis_index("wide")
     incoming, here = exchange(amplitude, tilt, owner, row_offset, col_offset)
-    plane = place(incoming)
-    bands = plane.shape[0]
+    bands = incoming.shape[0]
     scale = 1.0 / math.sqrt(TH * TW)
 
     most = bands - 1
@@ -151,11 +224,8 @@
     row_w = jnp.concatenate([weights, weights], axis=1)
     tables = (row_w[:, :, None] * fwd_h[None].astype(jnp.float32)).astype(jnp.bfloat16)
     tables = jnp.transpose(tables, (1, 0, 2)).reshape(2 * TH, bands * TH)
-    rows_r, rows_i = left_apply(tables, plane.reshape(bands * TH, 2 * TW))
     fwd_w = jnp.asarray(np.concatenate(dft_tables(TW, -1.0), axis=1))
-    pair = jnp.concatenate([rows_r, rows_i], axis=0).astype(jnp.bfloat16)
-    spec_r, spec_i = right_apply(pair, fwd_w)
-    spectrum = (jnp.stack([spec_r, spec_i]) * scale).astype(jnp.bfloat16)
+    spectrum = forward(incoming, tables, fwd_w)
 
     rows = TH // wide_count
     parts = lax.all_to_all(

time: 133 us -> 93.7 us (0.70)
  local copies, waits for them, and re-layouts: 42.9 us -> 8.61 us
  Pallas kernels: 0 us -> 23.4 us
  matrix products: 23 us -> 2.65 us
  waiting for transfers between devices: 23.3 us -> 15.8 us
    reshape x2 -> x1, local copies, waits for them, and re-layouts: 27.2 us -> 0.84 us  [local(): spectrum.reshape(2, wide_count, rows, TW)]
    pallas_call x0 -> x2, Pallas kernels: none -> 23.4 us  [the longest x1 21.4 us: forward(): pl.pallas_call(functools.partial(forward_kernel, bands, slots), out_shape...]
    dot_general x4 -> x2, matrix products: 15.7 us -> 1.21 us  [dot(): return jnp.dot(a, b, preferred_element_type=jnp.float32)]
    convert_element_type x1 -> x0, local copies, waits for them, and re-layouts: 11.5 us -> none  [place(): spread = jnp.einsum('bscuv,bsvx->bsucx', fields, col_hot, preferred_eleme...]
    all_to_all x1, waiting for transfers between devices: 14.6 us -> 6.98 us  [exchange(): lax.all_to_all(outgoing.reshape(bands, wide_count, slot_count, WORDS), 'w...]
    dot_general x1 -> x0, matrix products: 5.82 us -> none  [place(): jnp.einsum('bscuv,bsvx->bsucx', fields, col_hot, preferred_element_type=j...]
    unnamed x19 -> x23, local copies, waits for them, and re-layouts: 0.17 us -> 3.99 us
    convert_element_type x4 -> x2, other arithmetic: 2.12 us -> 3.99 us  [the longest x1 3.29 us: local(): (row_w[:, :, None] * fwd_h[None].astype(jnp.float32)).astype(jnp.bfloat16)]
  transfers between devices with their start and end apart: 2 -> 2, of which waited for: 2 -> 2; matrix products, arithmetic and copies ran while one was open for 1% -> 9% of each run, Pallas kernels for 0% -> 0%
where the time goes in v2:
time: 93.7 us; the launch traced here: 93.1 us
  blocking collectives  28.2 us (30%)
  Pallas kernels  23.4 us (25%)
  waiting for transfers between devices  15.8 us (17%)
  local copies, waits for them, and re-layouts  8.61 us (9%)
  starting transfers between devices  7.22 us (8%)
  other arithmetic  6.88 us (7%)
  matrix products  2.65 us (3%)
    pallas_call x1, Pallas kernels, forward(): pl.pallas_call(functools.partial(forward_kernel, bands, slots), out_shape...  21.4 us
    all_gather x1, blocking collectives, exchange(): packed = lax.all_gather(packed, 'narrow', axis=0, tiled=False)  16 us
    all_to_all x1, blocking collectives, local(): lax.all_to_all(focus, 'wide', split_axis=1, concat_axis=1, tiled=True)  12.2 us
    all_to_all x1, waiting for transfers between devices, local(): lax.all_to_all(spectrum.reshape(2, wide_count, rows, TW), 'wide', split_a...  8.78 us
    all_to_all x1, waiting for transfers between devices, exchange(): lax.all_to_all(outgoing.reshape(bands, wide_count, slot_count, WORDS), 'w...  6.98 us
    unnamed x23, local copies, waits for them, and re-layouts  3.99 us
    all_to_all x1, starting transfers between devices, exchange(): lax.all_to_all(outgoing.reshape(bands, wide_count, slot_count, WORDS), 'w...  3.73 us
    all_to_all x1, starting transfers between devices, local(): lax.all_to_all(spectrum.reshape(2, wide_count, rows, TW), 'wide', split_a...  3.49 us
  transfers between devices with their start and end apart: 2, of which 2 were waited for; matrix products, arithmetic and copies ran while one was open for 9% of the time, Pallas kernels for 0%

profile of v2, /device:TPU:0, one launch (start us, length us, event | category | flops | bytes accessed | tf_op | source)
XLA Modules:
  0.0 93.1 jit_solution(13783641383974610194)
XLA Ops:
  0.0 0.7 add_convert_fusion.1
  0.7 0.7 pad_maximum_fusion.1
  1.4 0.1 copy.33
  1.5 0.6 pad.8.par_ref
  2.1 2.1 %shard_map.181 = bf16[64,640]{1,0:T(8,128)(2,1)} custom-call(f32[64,256]{1,0:T(8,128)} %amp_ref.1, f32[64,8]{1,0:T(8,128)} %pad.8.par_ref), custom_call_target="tpu_custom_call" | custom-call | tf_op jit(solution)/shard_map/pallas_call | solution.py:80
  4.2 16.0 %all-gather = bf16[256,640]{1,0:T(8,128)(2,1)S(1)} all-gather(bf16[64,640]{1,0:T(8,128)(2,1)} %shard_map.181), channel_id=2, replica_groups=mesh['wide'=8,'narrow'=4] {'narrow'}, dimensions={0}, use_global_device_ids=true | all-gather | bytes 409600 | tf_op jit(solution)/shard_map/all_gather | solution.py:111
  20.2 0.2 convert_reduce_fusion
  20.4 0.9 fusion.1
  21.3 0.6 convolution_convert_fusion
  21.9 1.0 %copy.34 = bf16[4,8,24,640]{3,2,0,1:T(8,128)(2,1)} copy(bf16[4,8,24,640]{3,2,1,0:T(8,128)(2,1)S(1)} %bitcast.33) | data formatting | bytes 1966080 | tf_op jit(solution)/shard_map/reshape | solution.py:129
  23.0 3.7 %all-to-all-start = ((bf16[4,8,24,640]{3,2,0,1:T(8,128)(2,1)}), bf16[4,8,24,640]{3,2,0,1:T(8,128)(2,1)S(1)}, u32[]{:S(2)}, u32[]{:S(2)}) async-start(bf16[4,8,24,640]{3,2,0,1:T(8,128)(2,1)} %copy.34), calls=%async_computation | async-start | bytes 1966080 | tf_op jit(solution)/shard_map/all_to_all | solution.py:128
  26.7 1.0 %copy.36 = f32[1024,4]{1,0:T(8,128)} copy(f32[1024,4]{0,1:T(4,128)S(1)} %maximum_bitcast_fusion) | data formatting | bytes 32768 | tf_op jit(solution)/shard_map/mul | solution.py:225
  27.7 3.3 %multiply_convert_fusion = bf16[1024,4,512]{2,1,0:T(4,128)(2,1)S(1)} fusion(f32[1024,512]{1,0:T(8,128)S(1)} %copy-done.2, f32[1024,4]{1,0:T(8,128)} %copy.36), kind=kLoop, calls=%fused_computation | loop fusion | flops 4194304 | bytes 6307840 | tf_op jit(solution)/shard_map/convert_element_type | solution.py:225
  31.1 3.4 %copy.39 = bf16[128,8,4,512]{3,1,2,0:T(8,128)(2,1)} copy(bf16[128,8,4,512]{3,2,1,0:T(4,128)(2,1)S(1)} %bitcast.32) | data formatting | bytes 8388608
  34.4 7.0 %all-to-all-done = bf16[4,8,24,640]{3,2,0,1:T(8,128)(2,1)S(1)} async-done(((bf16[4,8,24,640]{3,2,0,1:T(8,128)(2,1)}), bf16[4,8,24,640]{3,2,0,1:T(8,128)(2,1)S(1)}, u32[]{:S(2)}, u32[]{:S(2)}) %all-to-all-start) | async-done | bytes 983072 | tf_op jit(solution)/shard_map/all_to_all | solution.py:128
  41.4 0.1 copy.35
  41.5 21.4 %shard_map.182 = bf16[2,512,256]{2,1,0:T(8,128)(2,1)S(1)} custom-call(bf16[768,640]{1,0:T(8,128)(2,1)S(1)} %bitcast.29, bf16[8,256,512]{2,1,0:T(8,128)(2,1)S(1)} %copy-done, bf16[1024,2048]{1,0:T(8,128)(2,1)} %bitcast.31, bf16[256,512]{1,0:T(8,128)(2,1)S(1)} %copy-done.1), custom_call_target="tpu_custom_call" | custom-call | tf_op jit(solution)/shard_map/pallas_call | solution.py:196
  63.0 0.8 copy.37
  63.8 3.5 %all-to-all-start.1 = ((bf16[2,8,64,256]{3,2,0,1:T(8,128)(2,1)}), bf16[2,8,64,256]{3,2,0,1:T(8,128)(2,1)S(1)}, u32[]{:S(2)}, u32[]{:S(2)}) async-start(bf16[2,8,64,256]{3,2,0,1:T(8,128)(2,1)} %copy.37), calls=%async_computation.1 | async-start | bytes 1048576 | tf_op jit(solution)/shard_map/all_to_all | solution.py:231
  67.3 0.9 constant_dynamic-slice_fusion
  68.2 8.8 %all-to-all-done.1 = bf16[2,8,64,256]{3,2,0,1:T(8,128)(2,1)S(1)} async-done(((bf16[2,8,64,256]{3,2,0,1:T(8,128)(2,1)}), bf16[2,8,64,256]{3,2,0,1:T(8,128)(2,1)S(1)}, u32[]{:S(2)}, u32[]{:S(2)}) %all-to-all-start.1) | async-done | bytes 524320 | tf_op jit(solution)/shard_map/all_to_all | solution.py:231
  77.0 0.1 convert_element_type.52
  77.1 0.3 fusion.6
  77.4 0.2 subtract_convert_fusion
  77.6 0.1 pad_maximum_fusion
  77.7 12.2 %all_to_all.15 = bf16[2,8,64,256]{3,2,0,1:T(8,128)(2,1)S(1)} all-to-all(bf16[2,8,64,256]{3,2,0,1:T(8,128)(2,1)S(1)} %pad_maximum_fusion), channel_id=1, replica_groups=mesh['wide'=8,'narrow'=4] {'wide'}, dimensions={1} | all-to-all | bytes 1048576 | tf_op jit(solution)/shard_map/all_to_all | solution.py:251
  89.9 0.5 fusion.22
  90.4 0.2 fusion.13
  90.6 0.6 copy-done.3
  91.1 0.7 fusion.14
  91.9 0.1 fusion.11
  92.0 1.1 %maximum_multiply_fusion = f32[2,512,256]{2,1,0:T(8,128)} fusion(f32[1,512,256]{2,1,0:T(8,128)S(1)} %get-tuple-element.8, f32[1,512,256]{2,1,0:T(8,128)S(1)} %get-tuple-element.7), kind=kLoop, calls=%fused_computation.17 | loop fusion | flops 524288 | bytes 2097152 | tf_op jit(solution)/shard_map/mul | solution.py:257
  (25 shorter events, 0.1 us)
Async XLA Ops:
  21.9 4.8 %copy-start.5 = (f32[7,512]{1,0:T(8,128)S(1)}, f32[7,512]{1,0:T(8,128)}, u32[]{:S(2)}) copy-start(f32[7,512]{1,0:T(8,128)} %constant.59.clone) | copy-start | bytes 43012
  21.9 5.8 %copy-start.2 = (f32[1024,512]{1,0:T(8,128)S(1)}, f32[1024,512]{1,0:T(8,128)}, u32[]{:S(2)}) copy-start(f32[1024,512]{1,0:T(8,128)} %constant.76) | copy-start | bytes 6291460
  23.0 18.4 %all-to-all-start = ((bf16[4,8,24,640]{3,2,0,1:T(8,128)(2,1)}), bf16[4,8,24,640]{3,2,0,1:T(8,128)(2,1)S(1)}, u32[]{:S(2)}, u32[]{:S(2)}) async-start(bf16[4,8,24,640]{3,2,0,1:T(8,128)(2,1)} %copy.34), calls=%async_computation | async-start | bytes 1966080 | tf_op jit(solution)/shard_map/all_to_all | solution.py:128
  31.0 10.5 %copy-start = (bf16[8,256,512]{2,1,0:T(8,128)(2,1)S(1)}, bf16[8,256,512]{2,1,0:T(8,128)(2,1)}, u32[]{:S(2)}) copy-start(bf16[8,256,512]{2,1,0:T(8,128)(2,1)} %constant.62.clone.tile_ref) | copy-start | bytes 6291460
  34.4 7.1 %copy-start.1 = (bf16[256,512]{1,0:T(8,128)(2,1)S(1)}, bf16[256,512]{1,0:T(8,128)(2,1)}, u32[]{:S(2)}) copy-start(bf16[256,512]{1,0:T(8,128)(2,1)} %constant.61.clone.wide_ref) | copy-start | bytes 786436
  62.9 14.2 %copy-start.6 = (f32[256]{0:T(256)S(1)}, f32[256]{0:T(256)}, u32[]{:S(2)}) copy-start(f32[256]{0:T(256)} %constant.63.clone) | copy-start | bytes 3076
  62.9 14.2 %copy-start.7 = (f32[256]{0:T(256)S(1)}, f32[256]{0:T(256)}, u32[]{:S(2)}) copy-start(f32[256]{0:T(256)} %constant.64.clone) | copy-start | bytes 3076
  62.9 14.2 %copy-start.8 = (f32[256]{0:T(256)S(1)}, f32[256]{0:T(256)}, u32[]{:S(2)}) copy-start(f32[256]{0:T(256)} %constant.65.clone) | copy-start | bytes 3076
  62.9 14.2 %copy-start.9 = (f32[256]{0:T(256)S(1)}, f32[256]{0:T(256)}, u32[]{:S(2)}) copy-start(f32[256]{0:T(256)} %constant.66.clone) | copy-start | bytes 3076
  63.0 14.2 %copy-start.10 = (f32[256]{0:T(256)S(1)}, f32[256]{0:T(256)}, u32[]{:S(2)}) copy-start(f32[256]{0:T(256)} %constant.67.clone) | copy-start | bytes 3076
  63.8 13.2 %all-to-all-start.1 = ((bf16[2,8,64,256]{3,2,0,1:T(8,128)(2,1)}), bf16[2,8,64,256]{3,2,0,1:T(8,128)(2,1)S(1)}, u32[]{:S(2)}, u32[]{:S(2)}) async-start(bf16[2,8,64,256]{3,2,0,1:T(8,128)(2,1)} %copy.37), calls=%async_computation.1 | async-start | bytes 1048576 | tf_op jit(solution)/shard_map/all_to_all | solution.py:231
  77.4 12.4 %copy-start.4 = (bf16[256,512]{1,0:T(8,128)(2,1)S(1)}, bf16[256,512]{1,0:T(8,128)(2,1)}, u32[]{:S(2)}) copy-start(bf16[256,512]{1,0:T(8,128)(2,1)} %constant.70.clone) | copy-start | bytes 786436
  89.9 1.2 %copy-start.3 = (bf16[1024,512]{1,0:T(8,128)(2,1)S(1)}, bf16[1024,512]{1,0:T(8,128)(2,1)}, u32[]{:S(2)}) copy-start(bf16[1024,512]{1,0:T(8,128)(2,1)} %constant.71.clone) | copy-start | bytes 3145732

commit v3 on v2

--- a/solution.py
+++ b/solution.py
@@ -40,7 +40,7 @@
     return (DEPTH * frequency * frequency % (2 * length * length)) * (-math.pi / (length * length))
 
 
-def render_kernel(amp_ref, par_ref, out_ref):
+def render_into(amp_ref, par_ref, out_ref):
     par = par_ref[...]
     tilt_r, tilt_c, lead = par[:, 0:1], par[:, 1:2], par[:, 2:3]
     owner, row_at, col_at = par[:, 3:4], par[:, 4:5], par[:, 5:6]
@@ -72,67 +72,163 @@
     out_ref[:, 4 * half :] = marks.astype(jnp.bfloat16)
 
 
-def render(amplitude, tilt, owner, row_offset, col_offset):
+MESH = pl.DeviceIdType.MESH
+
+
+def greet(targets):
+    barrier = pltpu.get_barrier_semaphore()
+    for valid, target in targets:
+        if valid is True:
+            pl.semaphore_signal(barrier, inc=1, device_id=target, device_id_type=MESH)
+        else:
+
+            @pl.when(valid)
+            def _():
+                pl.semaphore_signal(barrier, inc=1, device_id=target, device_id_type=MESH)
+
+    count = 0
+    for valid, _ in targets:
+        count = count + (1 if valid is True else valid.astype(jnp.int32))
+    pl.semaphore_wait(barrier, count)
+
+
+def front_kernel(
+    wide, narrow, bands, per, amp_ref, par_ref, out_ref, gathered, outgoing, incoming, send_n, recv_n, send_w, recv_w
+):
+    column, band = lax.axis_index("wide"), lax.axis_index("narrow")
+    block = outgoing.shape[1]
+
+    def first_of(where):
+        return jnp.clip(where - REACH, 0, narrow - bands)
+
+    first = first_of(band)
+    deltas = [d for d in range(-REACH, REACH + 1) if d != 0]
+    targets = [((band + d >= 0) & (band + d < narrow), (column, band + d)) for d in deltas]
+    peers = [(True, (lax.rem(column + step, wide), band)) for step in range(1, wide)]
+    greet(targets + peers)
+    render_into(amp_ref, par_ref, gathered.at[band - first])
+
+    def narrow_copy(k):
+        there = jnp.clip(band + deltas[k], 0, narrow - 1)
+        return pltpu.make_async_remote_copy(
+            src_ref=gathered.at[band - first],
+            dst_ref=gathered.at[jnp.clip(band - first_of(there), 0, bands - 1)],
+            send_sem=send_n.at[k],
+            recv_sem=recv_n.at[k],
+            device_id=(column, there),
+            device_id_type=MESH,
+        )
+
+    for k in range(len(deltas)):
+
+        @pl.when(targets[k][0])
+        def _(k=k):
+            narrow_copy(k).start()
+
+    for i in range(bands):
+        away = first + i - band
+
+        @pl.when((away > REACH) | (away < -REACH))
+        def _(i=i):
+            gathered[i] = jnp.zeros(gathered.shape[1:], gathered.dtype)
+
+    for k, d in enumerate(deltas):
+
+        @pl.when((band - d >= 0) & (band - d < narrow))
+        def _(k=k):
+            narrow_copy(k).wait_recv()
+
+    facets = amp_ref.shape[0]
+    lane = lax.broadcasted_iota(jnp.int32, (facets, 128), 1)
+    below = lax.broadcasted_iota(jnp.int32, (facets, facets), 0) > lax.broadcasted_iota(
+        jnp.int32, (facets, facets), 1
+    )
+    earlier = jnp.where(below, 1.0, 0.0).astype(jnp.bfloat16)
+    select = jnp.where(lax.broadcasted_iota(jnp.int32, (8, 128), 1) == 0, 1.0, 0.0).astype(jnp.bfloat16)
+    spot = lax.broadcasted_iota(jnp.int32, (wide * per, facets), 0).astype(jnp.float32)
+    sorted_by_owner = []
+    for i in range(bands):
+        packed = gathered[i]
+        owner = packed[:, 2 * PIXELS :].astype(jnp.float32)[:, 0:1]
+        chosen = jnp.where(lane.astype(jnp.float32) == owner, 1.0, 0.0)
+        rank = jnp.sum(dot(earlier, chosen.astype(jnp.bfloat16)) * chosen, axis=1, keepdims=True)
+        slot = jnp.where(lane == 0, owner * float(per) + rank, 0.0).astype(jnp.bfloat16)
+        slot = lax.dot_general(
+            select, slot, (((1,), (1,)), ((), ())), preferred_element_type=jnp.float32
+        )[0:1]
+        pick = jnp.where(spot == slot, 1.0, 0.0).astype(jnp.bfloat16)
+        sorted_by_owner.append(dot(pick, packed))
+    spare = block - bands * per
+    for w in range(wide):
+        pieces = [one[w * per : (w + 1) * per] for one in sorted_by_owner]
+        if spare:
+            pieces.append(jnp.zeros((spare, WORDS), jnp.float32))
+        outgoing[w] = jnp.concatenate(pieces, axis=0).astype(jnp.bfloat16)
+
+    def wide_copy(step):
+        there = lax.rem(column + step, wide)
+        return pltpu.make_async_remote_copy(
+            src_ref=outgoing.at[there],
+            dst_ref=incoming.at[column],
+            send_sem=send_w.at[step],
+            recv_sem=recv_w.at[step],
+            device_id=(there, band),
+            device_id_type=MESH,
+        )
+
+    for step in range(1, wide):
+        wide_copy(step).start()
+    incoming[column] = outgoing[column]
+    for step in range(1, wide):
+        wide_copy(step).wait_recv()
+    blocks = [incoming[w].astype(jnp.float32) for w in range(wide)]
+    for i in range(bands):
+        rows = jnp.concatenate([one[i * per : (i + 1) * per] for one in blocks], axis=0)
+        out_ref[i * wide * per : (i + 1) * wide * per, :] = rows.astype(jnp.bfloat16)
+    for step in range(1, wide):
+        wide_copy(step).wait_send()
+    for k in range(len(deltas)):
+
+        @pl.when(targets[k][0])
+        def _(k=k):
+            narrow_copy(k).wait_send()
+
+
+def exchange(amplitude, tilt, owner, row_offset, col_offset):
+    wide, narrow = lax.axis_size("wide"), lax.axis_size("narrow")
+    band = lax.axis_index("narrow")
+    facets = amplitude.shape[0]
+    per = max(2, (3 * facets + wide - 1) // wide)
+    bands = min(narrow, 2 * REACH + 1)
+    block = (bands * per + 15) // 16 * 16
     par = jnp.concatenate(
         [tilt, jnp.stack([owner[:, 0], row_offset, col_offset]).astype(jnp.float32)], axis=0
     )
     par = jnp.pad(par.T, ((0, 0), (0, 2)))
-    return pl.pallas_call(
-        render_kernel,
-        out_shape=jax.ShapeDtypeStruct((amplitude.shape[0], WORDS), jnp.bfloat16),
+    incoming = pl.pallas_call(
+        functools.partial(front_kernel, wide, narrow, bands, per),
+        out_shape=jax.ShapeDtypeStruct((bands * wide * per, WORDS), jnp.bfloat16),
+        in_specs=[pl.BlockSpec(memory_space=pltpu.VMEM)] * 2,
+        out_specs=pl.BlockSpec(memory_space=pltpu.VMEM),
+        scratch_shapes=[
+            pltpu.VMEM((bands, facets, WORDS), jnp.bfloat16),
+            pltpu.VMEM((wide, block, WORDS), jnp.bfloat16),
+            pltpu.VMEM((wide, block, WORDS), jnp.bfloat16),
+            pltpu.SemaphoreType.DMA((2 * REACH,)),
+            pltpu.SemaphoreType.DMA((2 * REACH,)),
+            pltpu.SemaphoreType.DMA((wide,)),
+            pltpu.SemaphoreType.DMA((wide,)),
+        ],
+        compiler_params=pltpu.CompilerParams(
+            collective_id=0, has_side_effects=True, vmem_limit_bytes=32 * 2**20
+        ),
     )(amplitude, par)
+    first = jnp.clip(band - REACH, 0, narrow - bands)
+    return incoming.reshape(bands, wide * per, WORDS), band - first
 
 
 def dot(a, b):
     return jnp.dot(a, b, preferred_element_type=jnp.float32)
-
-
-def left_apply(table, pair):
-    both = dot(table, pair)
-    half, wide = table.shape[0] // 2, pair.shape[1] // 2
-    top, low = both[:half], both[half:]
-    return top[:, :wide] - low[:, wide:], top[:, wide:] + low[:, :wide]
-
-
-def right_apply(pair, table):
-    both = dot(pair, table)
-    half, wide = pair.shape[0] // 2, table.shape[1] // 2
-    top, low = both[:half], both[half:]
-    return top[:, :wide] - low[:, wide:], top[:, wide:] + low[:, :wide]
-
-
-def exchange(amplitude, tilt, owner, row_offset, col_offset):
-    wide_count, narrow_count = lax.axis_size("wide"), lax.axis_size("narrow")
-    band = lax.axis_index("narrow")
-    facet_count = amplitude.shape[0]
-    slot_count = max(2, (3 * facet_count + wide_count - 1) // wide_count)
-    total_slots = wide_count * slot_count
-    packed = render(amplitude, tilt, owner, row_offset, col_offset)
-    packed = lax.all_gather(packed, "narrow", axis=0, tiled=False)
-    bands = min(narrow_count, 2 * REACH + 1)
-    first = jnp.clip(band - REACH, 0, narrow_count - bands)
-    if bands < narrow_count:
-        packed = lax.dynamic_slice_in_dim(packed, first, bands, 0)
-    target = packed[:, :, 2 * PIXELS].astype(jnp.int32)
-    chosen = target[:, :, None] == jnp.arange(wide_count, dtype=jnp.int32)[None, None, :]
-    earlier = jnp.asarray(np.tril(np.ones((facet_count, facet_count), np.float32), -1), jnp.bfloat16)
-    rank = jnp.einsum(
-        "fg,bgc->bfc", earlier, chosen.astype(jnp.bfloat16), preferred_element_type=jnp.float32
-    )
-    rank = jnp.sum(jnp.where(chosen, rank, 0.0), axis=2).astype(jnp.int32)
-    slot_at = target * slot_count + rank
-    pick = slot_at[:, None, :] == jnp.arange(total_slots, dtype=jnp.int32)[None, :, None]
-    outgoing = jnp.einsum(
-        "bsf,bfp->bsp", pick.astype(jnp.bfloat16), packed, preferred_element_type=jnp.float32
-    ).astype(jnp.bfloat16)
-    incoming = lax.all_to_all(
-        outgoing.reshape(bands, wide_count, slot_count, WORDS),
-        "wide",
-        split_axis=1,
-        concat_axis=1,
-        tiled=True,
-    )
-    return incoming.reshape(bands, total_slots, WORDS), band - first
 
 
 def forward_kernel(bands, slots, pay_ref, tile_ref, tab_ref, wide_ref, out_ref, mask, spread, plane, total):
@@ -179,8 +275,12 @@
     real = (total[:TH, :TW] - total[TH:, TW:]).astype(jnp.bfloat16)
     imag = (total[:TH, TW:] + total[TH:, :TW]).astype(jnp.bfloat16)
     by_real, by_imag = dot(real, wide_ref[...]), dot(imag, wide_ref[...])
-    out_ref[0] = ((by_real[:, :TW] - by_imag[:, TW:]) * scale).astype(jnp.bfloat16)
-    out_ref[1] = ((by_real[:, TW:] + by_imag[:, :TW]) * scale).astype(jnp.bfloat16)
+    spec_r = (by_real[:, :TW] - by_imag[:, TW:]) * scale
+    spec_i = (by_real[:, TW:] + by_imag[:, :TW]) * scale
+    wide, rows = out_ref.shape[0], out_ref.shape[1] // 2
+    for w in range(wide):
+        here = slice(w * rows, (w + 1) * rows)
+        out_ref[w] = jnp.concatenate([spec_r[here], spec_i[here]], axis=0).astype(jnp.bfloat16)
 
 
 def tile_tables():
@@ -191,11 +291,11 @@
     return same.astype(np.float32).astype(jnp.bfloat16)
 
 
-def forward(incoming, tables, fwd_w):
+def forward(incoming, tables, fwd_w, wide):
     bands, slots, _ = incoming.shape
     return pl.pallas_call(
         functools.partial(forward_kernel, bands, slots),
-        out_shape=jax.ShapeDtypeStruct((2, TH, TW), jnp.bfloat16),
+        out_shape=jax.ShapeDtypeStruct((wide, 2 * TH // wide, TW), jnp.bfloat16),
         scratch_shapes=[
             pltpu.VMEM((bands * slots, 2 * TW), jnp.float32),
             pltpu.VMEM((bands, FACET * slots, 2 * TW), jnp.bfloat16),
@@ -206,12 +306,101 @@
     )(incoming.reshape(bands * slots, WORDS), jnp.asarray(tile_tables()), tables, fwd_w)
 
 
+def back_kernel(
+    wide, spec_ref, weight_ref, phase_r_ref, phase_i_ref, wide_ref, high_ref, out_ref,
+    parts, focus, back, image, send_a, recv_a, send_b, recv_b,
+):
+    column, band = lax.axis_index("wide"), lax.axis_index("narrow")
+    rows = TH // wide
+    greet([(True, (lax.rem(column + step, wide), band)) for step in range(1, wide)])
+
+    def copy(step, source, landing, send, recv):
+        there = lax.rem(column + step, wide)
+        return pltpu.make_async_remote_copy(
+            src_ref=source.at[there],
+            dst_ref=landing.at[column],
+            send_sem=send.at[step],
+            recv_sem=recv.at[step],
+            device_id=(there, band),
+            device_id_type=MESH,
+        )
+
+    def out_copy(step):
+        return copy(step, spec_ref, parts, send_a, recv_a)
+
+    def home_copy(step):
+        return copy(step, focus, back, send_b, recv_b)
+
+    for step in range(1, wide):
+        out_copy(step).start()
+    parts[column] = spec_ref[column]
+    here = pl.ds(pl.multiple_of(column * rows, rows), rows)
+    phase_r, phase_i = phase_r_ref[here, :], phase_i_ref[here, :]
+    for step in range(1, wide):
+        out_copy(step).wait_recv()
+    for step in list(range(1, wide)) + [0]:
+        there = lax.rem(column + step, wide)
+        total = None
+        for offset in range(-REACH, REACH + 1):
+            source = there - offset
+            inside = jnp.where((source >= 0) & (source < wide), 1.0, 0.0)
+            weight = weight_ref[offset + REACH : offset + REACH + 1, :] * inside
+            term = weight * parts[jnp.clip(source, 0, wide - 1)].astype(jnp.float32)
+            total = term if total is None else total + term
+        real, imag = total[:rows], total[rows:]
+        turned = jnp.concatenate(
+            [phase_r * real - phase_i * imag, phase_r * imag + phase_i * real], axis=0
+        ).astype(jnp.bfloat16)
+        if step:
+            focus[there] = turned
+            home_copy(step).start()
+        else:
+            back[column] = turned
+    for step in range(wide):
+        source = lax.rem(column - step + wide, wide)
+        if step:
+            home_copy(step).wait_recv()
+        both = dot(back[source], wide_ref[...])
+        top, low = both[:rows], both[rows:]
+        image[source, :, :TW] = top[:, :TW] - low[:, TW:]
+        image[source, :, TW:] = top[:, TW:] + low[:, :TW]
+    scale = 1.0 / math.sqrt(TH * TW)
+    pair = image[...].reshape(TH, 2 * TW).astype(jnp.bfloat16)
+    top, low = dot(high_ref[:TH], pair), dot(high_ref[TH:], pair)
+    out_ref[0] = (top[:, :TW] - low[:, TW:]) * scale
+    out_ref[1] = (top[:, TW:] + low[:, :TW]) * scale
+    for step in range(1, wide):
+        out_copy(step).wait_send()
+        home_copy(step).wait_send()
+
+
+def backward(spectrum):
+    wide = spectrum.shape[0]
+    weight = np.zeros((8, TW), np.float32)
+    for offset in range(-REACH, REACH + 1):
+        weight[offset + REACH] = reach_weight(TW, float(offset))
+    angle = depth_phase(TH)[:, None] + depth_phase(TW)[None, :]
+    inv_w = np.concatenate(dft_tables(TW, 1.0), axis=1)
+    inv_h = np.concatenate(dft_tables(TH, 1.0), axis=0)
+    constants = [weight, np.cos(angle).astype(np.float32), np.sin(angle).astype(np.float32), inv_w, inv_h]
+    piece = pltpu.VMEM(spectrum.shape, jnp.bfloat16)
+    return pl.pallas_call(
+        functools.partial(back_kernel, wide),
+        out_shape=jax.ShapeDtypeStruct((2, TH, TW), jnp.float32),
+        in_specs=[pl.BlockSpec(memory_space=pltpu.VMEM)] * 6,
+        out_specs=pl.BlockSpec(memory_space=pltpu.VMEM),
+        scratch_shapes=[piece, piece, piece, pltpu.VMEM((wide, TH // wide, 2 * TW), jnp.float32)]
+        + [pltpu.SemaphoreType.DMA((wide,))] * 4,
+        compiler_params=pltpu.CompilerParams(
+            collective_id=1, has_side_effects=True, vmem_limit_bytes=32 * 2**20
+        ),
+    )(spectrum, *[jnp.asarray(one) for one in constants])
+
+
 def local(amplitude, tilt, owner, row_offset, col_offset):
     wide_count = lax.axis_size("wide")
-    column = lax.axis_index("wide")
     incoming, here = exchange(amplitude, tilt, owner, row_offset, col_offset)
     bands = incoming.shape[0]
-    scale = 1.0 / math.sqrt(TH * TW)
 
     most = bands - 1
     by_offset = np.zeros((2 * most + 1, TH), np.float32)
@@ -225,36 +414,7 @@
     tables = (row_w[:, :, None] * fwd_h[None].astype(jnp.float32)).astype(jnp.bfloat16)
     tables = jnp.transpose(tables, (1, 0, 2)).reshape(2 * TH, bands * TH)
     fwd_w = jnp.asarray(np.concatenate(dft_tables(TW, -1.0), axis=1))
-    spectrum = forward(incoming, tables, fwd_w)
-
-    rows = TH // wide_count
-    parts = lax.all_to_all(
-        spectrum.reshape(2, wide_count, rows, TW), "wide", split_axis=1, concat_axis=1, tiled=True
-    )
-    padded = jnp.pad(parts.astype(jnp.float32), ((0, 0), (REACH, REACH), (0, 0), (0, 0)))
-    total = 0.0
-    for offset in range(-REACH, REACH + 1):
-        start = REACH - offset
-        total = total + jnp.asarray(reach_weight(TW, float(offset))) * padded[
-            :, start : start + wide_count
-        ]
-    angle = depth_phase(TH)[:, None] + depth_phase(TW)[None, :]
-    phase_r = lax.dynamic_slice_in_dim(
-        jnp.asarray(np.cos(angle).astype(np.float32)), column * rows, rows, 0
-    )
-    phase_i = lax.dynamic_slice_in_dim(
-        jnp.asarray(np.sin(angle).astype(np.float32)), column * rows, rows, 0
-    )
-    focus = jnp.stack(
-        [phase_r * total[0] - phase_i * total[1], phase_r * total[1] + phase_i * total[0]]
-    ).astype(jnp.bfloat16)
-    focus = lax.all_to_all(focus, "wide", split_axis=1, concat_axis=1, tiled=True)
-    inv_w = jnp.asarray(np.concatenate(dft_tables(TW, 1.0), axis=1))
-    inv_h = jnp.asarray(np.concatenate(dft_tables(TH, 1.0), axis=0))
-    cols_r, cols_i = right_apply(focus.reshape(2 * TH, TW), inv_w)
-    pair = jnp.concatenate([cols_r, cols_i], axis=1).astype(jnp.bfloat16)
-    out_r, out_i = left_apply(inv_h, pair)
-    return jnp.stack([out_r, out_i]) * scale
+    return backward(forward(incoming, tables, fwd_w, wide_count))
 
 
 def solution(mesh):

time: 93.7 us -> 74.9 us (0.80)
  Pallas kernels: 23.4 us -> 64.7 us
  blocking collectives: 28.2 us -> 0 us
  waiting for transfers between devices: 15.8 us -> 0 us
  starting transfers between devices: 7.22 us -> 0 us
  other arithmetic: 6.88 us -> 3.63 us
  local copies, waits for them, and re-layouts: 8.61 us -> 5.46 us
  matrix products: 2.65 us -> 0 us
    pallas_call x1 -> x2, Pallas kernels: 2.06 us -> 43.2 us  [the longest x1 24.3 us: exchange(): pl.pallas_call(functools.partial(front_kernel, wide, narrow, bands, per),...]
    all_gather x1 -> x0, blocking collectives: 16 us -> none  [exchange(): packed = lax.all_gather(packed, 'narrow', axis=0, tiled=False)]
    all_to_all x2 -> x0, waiting for transfers between devices: 15.8 us -> none  [the longest x1 8.78 us: local(): lax.all_to_all(spectrum.reshape(2, wide_count, rows, TW), 'wide', split_a...]
    all_to_all x1 -> x0, blocking collectives: 12.2 us -> none  [local(): lax.all_to_all(focus, 'wide', split_axis=1, concat_axis=1, tiled=True)]
    all_to_all x2 -> x0, starting transfers between devices: 7.22 us -> none  [the longest x1 3.73 us: exchange(): lax.all_to_all(outgoing.reshape(bands, wide_count, slot_count, WORDS), 'w...]
    dot_general x4 -> x0, matrix products: 2.65 us -> none  [the longest x2 1.21 us: dot(): return jnp.dot(a, b, preferred_element_type=jnp.float32)]
    reshape x2 -> x0, local copies, waits for them, and re-layouts: 1.87 us -> none  [the longest x1 1.03 us: exchange(): outgoing.reshape(bands, wide_count, slot_count, WORDS)]
    mul x1 -> x0, other arithmetic: 1.06 us -> none  [local(): return jnp.stack([out_r, out_i]) * scale]
  transfers between devices with their start and end apart: 2 -> 0, of which waited for: 2 -> 0; matrix products, arithmetic and copies ran while one was open for 9% -> 0% of each run, Pallas kernels for 0% -> 0%
where the time goes in v3:
time: 74.9 us; the launch traced here: 74 us
  Pallas kernels  64.7 us (86%)
  local copies, waits for them, and re-layouts  5.46 us (7%)
  other arithmetic  3.63 us (5%)
    pallas_call x1, Pallas kernels, exchange(): pl.pallas_call(functools.partial(front_kernel, wide, narrow, bands, per),...  24.3 us
    pallas_call x1, Pallas kernels, forward(): pl.pallas_call(functools.partial(forward_kernel, bands, slots), out_shape...  21.5 us
    pallas_call x1, Pallas kernels, backward(): pl.pallas_call(functools.partial(back_kernel, wide), out_shape=jax.ShapeD...  18.8 us
    unnamed x26, local copies, waits for them, and re-layouts  4.41 us
    convert_element_type x1, other arithmetic, local(): (row_w[:, :, None] * fwd_h[None].astype(jnp.float32)).astype(jnp.bfloat16)  3.6 us

profile of v3, /device:TPU:0, one launch (start us, length us, event | category | flops | bytes accessed | tf_op | source)
XLA Modules:
  0.0 74.0 jit_solution(1970695832095930669)
XLA Ops:
  0.0 0.7 constant_dynamic-slice_fusion
  0.7 0.2 copy.20
  1.0 3.6 %multiply_convert_fusion = bf16[1024,4,512]{2,1,0:T(4,128)(2,1)S(1)} fusion(f32[1024,512]{1,0:T(8,128)} %constant.45, f32[1024,4]{1,0:T(8,128)S(1)} %copy.20), kind=kLoop, calls=%fused_computation | loop fusion | flops 4194304 | bytes 6307840 | tf_op jit(solution)/shard_map/convert_element_type | solution.py:414
  4.6 0.0 copy-start.9
  4.6 0.0 copy-start.10
  4.6 0.0 copy-start.11
  4.6 0.0 copy-start.8
  4.6 0.0 copy-start.6
  4.6 0.0 copy-start
  4.6 0.0 copy-start.4
  4.7 3.4 %copy.21 = bf16[128,8,4,512]{3,1,2,0:T(8,128)(2,1)} copy(bf16[128,8,4,512]{3,2,1,0:T(4,128)(2,1)S(1)} %bitcast.9) | data formatting | bytes 8388608
  8.0 0.0 copy-done.9
  8.0 0.0 copy-done.10
  8.0 0.0 copy-done.11
  8.0 0.0 copy-done.8
  8.1 0.1 copy.19
  8.2 0.0 copy-done.6
  8.2 24.3 %shard_map.136.pay_ref = bf16[768,640]{1,0:T(8,128)(2,1)S(1)} custom-call(f32[64,256]{1,0:T(8,128)S(1)} %copy-done.6, f32[64,8]{1,0:T(8,128)S(1)} %pad.4.par_ref), custom_call_target="tpu_custom_call" | custom-call | tf_op jit(solution)/shard_map/pallas_call | solution.py:208
  32.5 0.0 copy-done
  32.5 0.0 copy-done.4
  32.5 0.0 copy-start.1
  32.6 0.0 copy-start.2
  32.6 0.0 copy-start.3
  32.6 0.0 copy-start.5
  32.6 0.0 copy-start.7
  32.6 21.5 %shard_map.137.spec_ref = bf16[8,128,256]{2,1,0:T(8,128)(2,1)S(1)} custom-call(bf16[768,640]{1,0:T(8,128)(2,1)S(1)} %shard_map.136.pay_ref, bf16[8,256,512]{2,1,0:T(8,128)(2,1)S(1)} %copy-done, bf16[1024,2048]{1,0:T(8,128)(2,1)} %bitcast.8, bf16[256,512]{1,0:T(8,128)(2,1)S(1)} %copy-done.4), custom_call_target="tpu_custom_call" | custom-call | tf_op jit(solution)/shard_map/pallas_call | solution.py:296
  54.2 0.0 copy-done.1
  54.2 0.0 copy-done.2
  54.2 0.0 copy-done.3
  54.2 0.0 copy-done.5
  54.2 18.8 %shard_map.138 = f32[2,512,256]{2,1,0:T(8,128)S(1)} custom-call(bf16[8,128,256]{2,1,0:T(8,128)(2,1)S(1)} %shard_map.137.spec_ref, f32[8,256]{1,0:T(8,128)S(1)} %copy-done.7, f32[512,256]{1,0:T(8,128)S(1)} %copy-done.2, f32[512,256]{1,0:T(8,128)S(1)} %copy-done.3, bf16[256,512]{1,0:T(8,128)(2,1)S(1)} %copy-done.5, bf16[1024,512]{1,0:T(8,128)(2,1)S(1)} %copy-done.1), custom_call_target="tpu_custom_call" | custom-call | tf_op jit(solution)/shard_map/pallas_call | solution.py:387
  73.0 1.0 %copy.23 = f32[2,512,256]{2,1,0:T(8,128)} copy(f32[2,512,256]{2,1,0:T(8,128)S(1)} %shard_map.138) | data formatting | bytes 2097152
  (5 shorter events, 0.0 us)
Async XLA Ops:
  4.6 3.4 %copy-start.9 = (s32[64]{0:T(128)S(1)}, s32[64]{0:T(128)}, u32[]{:S(2)}) copy-start(s32[64]{0:T(128)} %param.18) | copy-start | bytes 772
  4.6 3.4 %copy-start.10 = (s32[64]{0:T(128)S(1)}, s32[64]{0:T(128)}, u32[]{:S(2)}) copy-start(s32[64]{0:T(128)} %param.17) | copy-start | bytes 772
  4.6 3.4 %copy-start.11 = (s32[64,1]{0,1:T(1,128)S(1)}, s32[64,1]{0,1:T(1,128)}, u32[]{:S(2)}) copy-start(s32[64,1]{0,1:T(1,128)} %param.16) | copy-start | bytes 772
  4.6 3.4 %copy-start.8 = (f32[3,64]{1,0:T(4,128)S(1)}, f32[3,64]{1,0:T(4,128)}, u32[]{:S(2)}) copy-start(f32[3,64]{1,0:T(4,128)} %param.15) | copy-start | bytes 2308
  4.6 3.6 %copy-start.6 = (f32[64,256]{1,0:T(8,128)S(1)}, f32[64,256]{1,0:T(8,128)}, u32[]{:S(2)}) copy-start(f32[64,256]{1,0:T(8,128)} %amp_ref.1) | copy-start | bytes 196612
  4.6 27.9 %copy-start = (bf16[8,256,512]{2,1,0:T(8,128)(2,1)S(1)}, bf16[8,256,512]{2,1,0:T(8,128)(2,1)}, u32[]{:S(2)}) copy-start(bf16[8,256,512]{2,1,0:T(8,128)(2,1)} %constant.37.clone.tile_ref) | copy-start | bytes 6291460
  4.6 27.9 %copy-start.4 = (bf16[256,512]{1,0:T(8,128)(2,1)S(1)}, bf16[256,512]{1,0:T(8,128)(2,1)}, u32[]{:S(2)}) copy-start(bf16[256,512]{1,0:T(8,128)(2,1)} %constant.36.clone.wide_ref) | copy-start | bytes 786436
  32.5 21.6 %copy-start.1 = (bf16[1024,512]{1,0:T(8,128)(2,1)S(1)}, bf16[1024,512]{1,0:T(8,128)(2,1)}, u32[]{:S(2)}) copy-start(bf16[1024,512]{1,0:T(8,128)(2,1)} %constant.42.clone.high_ref) | copy-start | bytes 3145732
  32.6 21.6 %copy-start.2 = (f32[512,256]{1,0:T(8,128)S(1)}, f32[512,256]{1,0:T(8,128)}, u32[]{:S(2)}) copy-start(f32[512,256]{1,0:T(8,128)} %constant.39.clone.phase_r_ref) | copy-start | bytes 1572868
  32.6 21.6 %copy-start.3 = (f32[512,256]{1,0:T(8,128)S(1)}, f32[512,256]{1,0:T(8,128)}, u32[]{:S(2)}) copy-start(f32[512,256]{1,0:T(8,128)} %constant.40.clone.phase_i_ref) | copy-start | bytes 1572868
  32.6 21.6 %copy-start.5 = (bf16[256,512]{1,0:T(8,128)(2,1)S(1)}, bf16[256,512]{1,0:T(8,128)(2,1)}, u32[]{:S(2)}) copy-start(bf16[256,512]{1,0:T(8,128)(2,1)} %constant.41.clone.wide_ref) | copy-start | bytes 786436
  32.6 21.6 %copy-start.7 = (f32[8,256]{1,0:T(8,128)S(1)}, f32[8,256]{1,0:T(8,128)}, u32[]{:S(2)}) copy-start(f32[8,256]{1,0:T(8,128)} %constant.38.clone.weight_ref) | copy-start | bytes 24580

commit v4 on v3

--- a/solution.py
+++ b/solution.py
@@ -92,8 +92,8 @@
     pl.semaphore_wait(barrier, count)
 
 
-def front_kernel(
-    wide, narrow, bands, per, amp_ref, par_ref, out_ref, gathered, outgoing, incoming, send_n, recv_n, send_w, recv_w
+def front(
+    wide, narrow, bands, per, meanwhile, amp_ref, par_ref, out_ref, gathered, outgoing, incoming, send_n, recv_n, send_w, recv_w
 ):
     column, band = lax.axis_index("wide"), lax.axis_index("narrow")
     block = outgoing.shape[1]
@@ -132,6 +132,7 @@
         def _(i=i):
             gathered[i] = jnp.zeros(gathered.shape[1:], gathered.dtype)
 
+    meanwhile()
     for k, d in enumerate(deltas):
 
         @pl.when((band - d >= 0) & (band - d < narrow))
@@ -194,55 +195,31 @@
             narrow_copy(k).wait_send()
 
 
-def exchange(amplitude, tilt, owner, row_offset, col_offset):
-    wide, narrow = lax.axis_size("wide"), lax.axis_size("narrow")
-    band = lax.axis_index("narrow")
-    facets = amplitude.shape[0]
-    per = max(2, (3 * facets + wide - 1) // wide)
-    bands = min(narrow, 2 * REACH + 1)
-    block = (bands * per + 15) // 16 * 16
-    par = jnp.concatenate(
-        [tilt, jnp.stack([owner[:, 0], row_offset, col_offset]).astype(jnp.float32)], axis=0
-    )
-    par = jnp.pad(par.T, ((0, 0), (0, 2)))
-    incoming = pl.pallas_call(
-        functools.partial(front_kernel, wide, narrow, bands, per),
-        out_shape=jax.ShapeDtypeStruct((bands * wide * per, WORDS), jnp.bfloat16),
-        in_specs=[pl.BlockSpec(memory_space=pltpu.VMEM)] * 2,
-        out_specs=pl.BlockSpec(memory_space=pltpu.VMEM),
-        scratch_shapes=[
-            pltpu.VMEM((bands, facets, WORDS), jnp.bfloat16),
-            pltpu.VMEM((wide, block, WORDS), jnp.bfloat16),
-            pltpu.VMEM((wide, block, WORDS), jnp.bfloat16),
-            pltpu.SemaphoreType.DMA((2 * REACH,)),
-            pltpu.SemaphoreType.DMA((2 * REACH,)),
-            pltpu.SemaphoreType.DMA((wide,)),
-            pltpu.SemaphoreType.DMA((wide,)),
-        ],
-        compiler_params=pltpu.CompilerParams(
-            collective_id=0, has_side_effects=True, vmem_limit_bytes=32 * 2**20
-        ),
-    )(amplitude, par)
-    first = jnp.clip(band - REACH, 0, narrow - bands)
-    return incoming.reshape(bands, wide * per, WORDS), band - first
-
-
 def dot(a, b):
     return jnp.dot(a, b, preferred_element_type=jnp.float32)
 
 
-def forward_kernel(bands, slots, pay_ref, tile_ref, tab_ref, wide_ref, out_ref, mask, spread, plane, total):
+def fill_tiles(tile_ref):
+    half = PIXELS // 2
+    lane = lax.broadcasted_iota(jnp.int32, tile_ref.shape[1:], 0)
+    spot = lax.broadcasted_iota(jnp.int32, tile_ref.shape[1:], 1)
+    same = (lane // half == spot // TW) & (lane % FACET == spot % FACET)
+    group = jnp.where(same, lane % half // FACET, -1)
+    for at in range(FACET // 2):
+        tile_ref[at] = jnp.where(group == at, 1.0, 0.0).astype(jnp.bfloat16)
+
+
+def forward(bands, slots, here, pay_ref, tile_ref, tab_ref, weight_ref, wide_ref, out_ref, mask, spread, plane, total):
     half = PIXELS
     marks = pay_ref[:, 2 * PIXELS :].astype(jnp.float32)
     col_at = FACET * marks[:, 3:4] + marks[:, 4:5]
     spot = (lax.broadcasted_iota(jnp.int32, mask.shape, 1) % TW).astype(jnp.float32) - col_at
-    mask[...] = jnp.where((spot >= 0.0) & (spot < FACET), 1.0, 0.0)
+    mask[...] = jnp.where((spot >= 0.0) & (spot < FACET), 1.0, 0.0).astype(jnp.bfloat16)
     for side in range(2):
         fields = pay_ref[:, side * half : (side + 1) * half]
 
         def widen(at, _):
-            pixels = dot(fields, tile_ref[at]) * mask[...]
-            pixels = pixels.astype(jnp.bfloat16)
+            pixels = dot(fields, tile_ref[at]).astype(jnp.bfloat16) * mask[...]
             row = pl.multiple_of((side * (FACET // 2) + at) * slots, slots)
             for b in range(bands):
                 spread[b, pl.ds(row, slots), :] = pixels[b * slots : (b + 1) * slots]
@@ -251,7 +228,7 @@
         lax.fori_loop(0, FACET // 2, widen, 0)
     lane = lax.broadcasted_iota(jnp.int32, (8, 128), 1)
     select = jnp.where(lane == 1, float(FACET), jnp.where(lane == 2, 1.0, 0.0)).astype(jnp.bfloat16)
-    group = 4
+    group = 8
     depth = group * slots
     spot = lax.broadcasted_iota(jnp.int32, (TH, depth), 0).astype(jnp.float32)
     for b in range(bands):
@@ -260,17 +237,17 @@
             select, corner, (((1,), (1,)), ((), ())), preferred_element_type=jnp.float32
         )[0:1]
         row_at = jnp.concatenate([row_at + float(u) for u in range(group)], axis=1)
-        plane[...] = jnp.zeros_like(plane)
-
-        def add_rows(at, _):
-            step = (at * group).astype(jnp.float32)
-            hot = jnp.where(spot == row_at + step, 1.0, 0.0).astype(jnp.bfloat16)
-            plane[...] += dot(hot, spread[b, pl.ds(pl.multiple_of(at * depth, depth), depth), :])
-            return 0
-
-        lax.fori_loop(0, FACET // group, add_rows, 0)
-        rows = dot(tab_ref[:, b * TH : (b + 1) * TH], plane[...].astype(jnp.bfloat16))
-        total[...] = rows if b == 0 else total[...] + rows
+        for at in range(FACET // group):
+            hot = jnp.where(spot == row_at + float(at * group), 1.0, 0.0).astype(jnp.bfloat16)
+            part = dot(hot, spread[b, at * depth : (at + 1) * depth, :])
+            plane[...] = part if at == 0 else plane[...] + part
+        place = lax.broadcasted_iota(jnp.int32, weight_ref.shape, 1) - 2 * REACH
+        weight = jnp.sum(jnp.where(place == here - b, weight_ref[...], 0.0), axis=1, keepdims=True)
+        source = plane[...].astype(jnp.bfloat16)
+        for part in range(2):
+            half = slice(part * TH, (part + 1) * TH)
+            rows = weight * dot(tab_ref[half, :], source)
+            total[half, :] = rows if b == 0 else total[half, :] + rows
     scale = 1.0 / math.sqrt(TH * TW)
     real = (total[:TH, :TW] - total[TH:, TW:]).astype(jnp.bfloat16)
     imag = (total[:TH, TW:] + total[TH:, :TW]).astype(jnp.bfloat16)
@@ -283,36 +260,12 @@
         out_ref[w] = jnp.concatenate([spec_r[here], spec_i[here]], axis=0).astype(jnp.bfloat16)
 
 
-def tile_tables():
-    lane = np.arange(PIXELS)[None, :, None]
-    spot = np.arange(2 * TW)[None, None, :]
-    at = np.arange(FACET // 2)[:, None, None]
-    same = (lane // 128 == spot // TW) & (lane % 128 == at * FACET + spot % FACET)
-    return same.astype(np.float32).astype(jnp.bfloat16)
-
-
-def forward(incoming, tables, fwd_w, wide):
-    bands, slots, _ = incoming.shape
-    return pl.pallas_call(
-        functools.partial(forward_kernel, bands, slots),
-        out_shape=jax.ShapeDtypeStruct((wide, 2 * TH // wide, TW), jnp.bfloat16),
-        scratch_shapes=[
-            pltpu.VMEM((bands * slots, 2 * TW), jnp.float32),
-            pltpu.VMEM((bands, FACET * slots, 2 * TW), jnp.bfloat16),
-            pltpu.VMEM((TH, 2 * TW), jnp.float32),
-            pltpu.VMEM((2 * TH, 2 * TW), jnp.float32),
-        ],
-        compiler_params=pltpu.CompilerParams(vmem_limit_bytes=48 * 2**20),
-    )(incoming.reshape(bands * slots, WORDS), jnp.asarray(tile_tables()), tables, fwd_w)
-
-
-def back_kernel(
-    wide, spec_ref, weight_ref, phase_r_ref, phase_i_ref, wide_ref, high_ref, out_ref,
+def backward(
+    wide, arrive, spec_ref, weight_ref, phase, wide_ref, high_ref, out_ref,
     parts, focus, back, image, send_a, recv_a, send_b, recv_b,
 ):
     column, band = lax.axis_index("wide"), lax.axis_index("narrow")
     rows = TH // wide
-    greet([(True, (lax.rem(column + step, wide), band)) for step in range(1, wide)])
 
     def copy(step, source, landing, send, recv):
         there = lax.rem(column + step, wide)
@@ -334,8 +287,8 @@
     for step in range(1, wide):
         out_copy(step).start()
     parts[column] = spec_ref[column]
-    here = pl.ds(pl.multiple_of(column * rows, rows), rows)
-    phase_r, phase_i = phase_r_ref[here, :], phase_i_ref[here, :]
+    arrive()
+    phase_r, phase_i = phase[0], phase[1]
     for step in range(1, wide):
         out_copy(step).wait_recv()
     for step in list(range(1, wide)) + [0]:
@@ -374,47 +327,110 @@
         home_copy(step).wait_send()
 
 
-def backward(spectrum):
-    wide = spectrum.shape[0]
-    weight = np.zeros((8, TW), np.float32)
+def whole_kernel(
+    wide, narrow, bands, per,
+    amp_ref, par_ref, row_weight, col_weight, fwd_w, inv_w, phase_all, fwd_h_all, inv_h_all, out_ref,
+    gathered, outgoing, incoming, send_n, recv_n, send_w, recv_w,
+    pay, tiles, mask, spread, plane, total, spec,
+    parts, focus, back, image, send_a, recv_a, send_b, recv_b,
+    phase, fwd_h, inv_h, load,
+):
+    column, band = lax.axis_index("wide"), lax.axis_index("narrow")
+    rows = TH // wide
+    own = pl.ds(pl.multiple_of(column * rows, rows), rows)
+    fetch_tab = pltpu.make_async_copy(fwd_h_all, fwd_h, load.at[0])
+    fetch_phase = pltpu.make_async_copy(phase_all.at[:, own, :], phase, load.at[1])
+    fetch_inv = pltpu.make_async_copy(inv_h_all, inv_h, load.at[2])
+    for one in (fetch_tab, fetch_phase, fetch_inv):
+        one.start()
+    front(
+        wide, narrow, bands, per, lambda: fill_tiles(tiles),
+        amp_ref, par_ref, pay, gathered, outgoing, incoming, send_n, recv_n, send_w, recv_w,
+    )
+    fetch_tab.wait()
+    here = band - jnp.clip(band - REACH, 0, narrow - bands)
+    forward(
+        bands, wide * per, here, pay, tiles, fwd_h, row_weight, fwd_w, spec, mask, spread, plane, total
+    )
+
+    def arrive():
+        fetch_phase.wait()
+        fetch_inv.wait()
+
+    backward(
+        wide, arrive, spec, col_weight, phase, inv_w, inv_h, out_ref,
+        parts, focus, back, image, send_a, recv_a, send_b, recv_b,
+    )
+
+
+def local(amplitude, tilt, owner, row_offset, col_offset):
+    wide, narrow = lax.axis_size("wide"), lax.axis_size("narrow")
+    facets = amplitude.shape[0]
+    per = max(2, (3 * facets + wide - 1) // wide)
+    bands = min(narrow, 2 * REACH + 1)
+    slots = wide * per
+    block = (bands * per + 15) // 16 * 16
+    rows = TH // wide
+    par = jnp.concatenate(
+        [tilt, jnp.stack([owner[:, 0], row_offset, col_offset]).astype(jnp.float32)], axis=0
+    )
+    par = jnp.pad(par.T, ((0, 0), (0, 2)))
+    row_weight = np.zeros((TH, 128), np.float32)
+    col_weight = np.zeros((8, TW), np.float32)
     for offset in range(-REACH, REACH + 1):
-        weight[offset + REACH] = reach_weight(TW, float(offset))
+        row_weight[:, 2 * REACH + offset] = reach_weight(TH, float(offset))
+        col_weight[offset + REACH] = reach_weight(TW, float(offset))
     angle = depth_phase(TH)[:, None] + depth_phase(TW)[None, :]
-    inv_w = np.concatenate(dft_tables(TW, 1.0), axis=1)
-    inv_h = np.concatenate(dft_tables(TH, 1.0), axis=0)
-    constants = [weight, np.cos(angle).astype(np.float32), np.sin(angle).astype(np.float32), inv_w, inv_h]
-    piece = pltpu.VMEM(spectrum.shape, jnp.bfloat16)
+    phase = np.stack([np.cos(angle), np.sin(angle)]).astype(np.float32)
+    constants = [
+        row_weight,
+        col_weight,
+        np.concatenate(dft_tables(TW, -1.0), axis=1),
+        np.concatenate(dft_tables(TW, 1.0), axis=1),
+        phase,
+        np.concatenate(dft_tables(TH, -1.0), axis=0),
+        np.concatenate(dft_tables(TH, 1.0), axis=0),
+    ]
+    dma = lambda count: pltpu.SemaphoreType.DMA((count,))
+    narrow16 = lambda *shape: pltpu.VMEM(shape, jnp.bfloat16)
+    wide32 = lambda *shape: pltpu.VMEM(shape, jnp.float32)
     return pl.pallas_call(
-        functools.partial(back_kernel, wide),
+        functools.partial(whole_kernel, wide, narrow, bands, per),
         out_shape=jax.ShapeDtypeStruct((2, TH, TW), jnp.float32),
-        in_specs=[pl.BlockSpec(memory_space=pltpu.VMEM)] * 6,
+        in_specs=[pl.BlockSpec(memory_space=pltpu.VMEM)] * 6 + [pl.BlockSpec(memory_space=pl.ANY)] * 3,
         out_specs=pl.BlockSpec(memory_space=pltpu.VMEM),
-        scratch_shapes=[piece, piece, piece, pltpu.VMEM((wide, TH // wide, 2 * TW), jnp.float32)]
-        + [pltpu.SemaphoreType.DMA((wide,))] * 4,
+        scratch_shapes=[
+            narrow16(bands, facets, WORDS),
+            narrow16(wide, block, WORDS),
+            narrow16(wide, block, WORDS),
+            dma(2 * REACH),
+            dma(2 * REACH),
+            dma(wide),
+            dma(wide),
+            narrow16(bands * slots, WORDS),
+            narrow16(FACET // 2, PIXELS, 2 * TW),
+            narrow16(bands * slots, 2 * TW),
+            narrow16(bands, FACET * slots, 2 * TW),
+            wide32(TH, 2 * TW),
+            wide32(2 * TH, 2 * TW),
+            narrow16(wide, 2 * rows, TW),
+            narrow16(wide, 2 * rows, TW),
+            narrow16(wide, 2 * rows, TW),
+            narrow16(wide, 2 * rows, TW),
+            wide32(wide, rows, 2 * TW),
+            dma(wide),
+            dma(wide),
+            dma(wide),
+            dma(wide),
+            wide32(2, rows, TW),
+            narrow16(2 * TH, TH),
+            narrow16(2 * TH, TH),
+            dma(3),
+        ],
         compiler_params=pltpu.CompilerParams(
-            collective_id=1, has_side_effects=True, vmem_limit_bytes=32 * 2**20
+            collective_id=0, has_side_effects=True, vmem_limit_bytes=56 * 2**20
         ),
-    )(spectrum, *[jnp.asarray(one) for one in constants])
-
-
-def local(amplitude, tilt, owner, row_offset, col_offset):
-    wide_count = lax.axis_size("wide")
-    incoming, here = exchange(amplitude, tilt, owner, row_offset, col_offset)
-    bands = incoming.shape[0]
-
-    most = bands - 1
-    by_offset = np.zeros((2 * most + 1, TH), np.float32)
-    for offset in range(-REACH, REACH + 1):
-        if abs(offset) <= most:
-            by_offset[offset + most] = reach_weight(TH, float(offset))
-    weights = lax.dynamic_slice_in_dim(jnp.asarray(by_offset[::-1].copy()), most - here, bands, 0)
-    fwd_hr, fwd_hi = dft_tables(TH, -1.0)
-    fwd_h = jnp.asarray(np.concatenate([fwd_hr, fwd_hi], axis=0))
-    row_w = jnp.concatenate([weights, weights], axis=1)
-    tables = (row_w[:, :, None] * fwd_h[None].astype(jnp.float32)).astype(jnp.bfloat16)
-    tables = jnp.transpose(tables, (1, 0, 2)).reshape(2 * TH, bands * TH)
-    fwd_w = jnp.asarray(np.concatenate(dft_tables(TW, -1.0), axis=1))
-    return backward(forward(incoming, tables, fwd_w, wide_count))
+    )(amplitude, par, *[jnp.asarray(one) for one in constants])
 
 
 def solution(mesh):

time: 74.9 us -> 65.1 us (0.87)
  Pallas kernels: 64.7 us -> 59.9 us
  other arithmetic: 3.63 us -> 0.02 us
  local copies, waits for them, and re-layouts: 5.46 us -> 4.34 us
    pallas_call x3 -> x1, Pallas kernels: 64.7 us -> 59.9 us  [local(): pl.pallas_call(functools.partial(whole_kernel, wide, narrow, bands, per),...]
    convert_element_type x2 -> x1, other arithmetic: 3.61 us -> 0.01 us  [local(): jnp.stack([owner[:, 0], row_offset, col_offset]).astype(jnp.float32)]
    unnamed x26 -> x9, local copies, waits for them, and re-layouts: 4.41 us -> 3.62 us
where the time goes in v4:
time: 65.1 us; the launch traced here: 64.3 us
  Pallas kernels  59.9 us (92%)
  local copies, waits for them, and re-layouts  4.34 us (7%)
    pallas_call x1, Pallas kernels, local(): pl.pallas_call(functools.partial(whole_kernel, wide, narrow, bands, per),...  59.9 us
    unnamed x9, local copies, waits for them, and re-layouts  3.62 us

profile of v4, /device:TPU:0, one launch (start us, length us, event | category | flops | bytes accessed | tf_op | source)
XLA Modules:
  0.0 64.3 jit_solution(12388300841886468209)
XLA Ops:
  0.0 0.0 copy-start.1
  0.0 0.0 copy-start.2
  0.0 0.0 copy-start.3
  0.0 0.6 %copy-done.1 = s32[64]{0:T(128)S(1)} copy-done((s32[64]{0:T(128)S(1)}, s32[64]{0:T(128)}, u32[]{:S(2)}) %copy-start.1) | copy-done | bytes 280
  0.7 0.0 copy-done.2
  0.7 0.0 copy-done.3
  0.7 0.0 copy-start
  0.7 0.7 %copy-done = f32[3,64]{1,0:T(4,128)S(1)} copy-done((f32[3,64]{1,0:T(4,128)S(1)}, f32[3,64]{1,0:T(4,128)}, u32[]{:S(2)}) %copy-start) | copy-done | bytes 792
  1.4 0.1 copy.17
  1.5 0.6 pad.4.par_ref
  2.1 59.9 %shard_map.118 = f32[2,512,256]{2,1,0:T(8,128)} custom-call(f32[64,256]{1,0:T(8,128)} %amp_ref.1, f32[64,8]{1,0:T(8,128)} %pad.4.par_ref, f32[512,128]{1,0:T(8,128)} %constant.17.clone.row_weight, f32[8,256]{1,0:T(8,128)} %constant.18.clone.col_weight, bf16[256,512]{1,0:T(8,128)(2,1)} %constant.19.clone.fwd_w, bf16[256,512]{1,0:T(8,128)(2,1)} %constant.20.clone.inv_w, ...), custom_call_target="tpu_custom_call" | custom-call | tf_op jit(solution)/shard_map/pallas_call | solution.py:397
  62.0 2.3 %copy.19 = f32[2,512,256]{2,1,0:T(8,128)} copy(f32[2,512,256]{2,1,0:T(8,128)} %shard_map.118) | data formatting | bytes 2097152
  (2 shorter events, 0.0 us)
Async XLA Ops:
  0.0 0.7 %copy-start.1 = (s32[64]{0:T(128)S(1)}, s32[64]{0:T(128)}, u32[]{:S(2)}) copy-start(s32[64]{0:T(128)} %param.16) | copy-start | bytes 772
  0.0 0.7 %copy-start.2 = (s32[64]{0:T(128)S(1)}, s32[64]{0:T(128)}, u32[]{:S(2)}) copy-start(s32[64]{0:T(128)} %param.15) | copy-start | bytes 772
  0.0 0.7 %copy-start.3 = (s32[64,1]{0,1:T(1,128)S(1)}, s32[64,1]{0,1:T(1,128)}, u32[]{:S(2)}) copy-start(s32[64,1]{0,1:T(1,128)} %param.14) | copy-start | bytes 772
  0.7 0.7 %copy-start = (f32[3,64]{1,0:T(4,128)S(1)}, f32[3,64]{1,0:T(4,128)}, u32[]{:S(2)}) copy-start(f32[3,64]{1,0:T(4,128)} %param.13) | copy-start | bytes 2308

commit v5 on v4

--- a/solution.py
+++ b/solution.py
@@ -16,7 +16,7 @@
 REACH = 2
 SPREAD = 16.0
 PIXELS = FACET * FACET
-WORDS = 2 * PIXELS + 128
+PARTS = (PIXELS + 128, PIXELS)
 
 
 def dft_tables(length, spin_sign):
@@ -40,7 +40,7 @@
     return (DEPTH * frequency * frequency % (2 * length * length)) * (-math.pi / (length * length))
 
 
-def render_into(amp_ref, par_ref, out_ref):
+def render_into(amp_ref, par_ref, low_ref, high_ref):
     par = par_ref[...]
     tilt_r, tilt_c, lead = par[:, 0:1], par[:, 1:2], par[:, 2:3]
     owner, row_at, col_at = par[:, 3:4], par[:, 4:5], par[:, 5:6]
@@ -61,15 +61,15 @@
     phase = tilt_r * (lane // FACET).astype(jnp.float32) + tilt_c * pixel + lead
     real, imag = (amp * jnp.cos(phase)).astype(jnp.bfloat16), (amp * jnp.sin(phase)).astype(jnp.bfloat16)
     half = PIXELS // 2
-    out_ref[:, 0:half] = real[:, :half]
-    out_ref[:, half : 2 * half] = imag[:, :half]
-    out_ref[:, 2 * half : 3 * half] = real[:, half:]
-    out_ref[:, 3 * half : 4 * half] = imag[:, half:]
+    low_ref[:, 0:half] = real[:, half:]
+    low_ref[:, half : 2 * half] = imag[:, half:]
+    high_ref[:, 0:half] = real[:, :half]
+    high_ref[:, half : 2 * half] = imag[:, :half]
     spot = lax.broadcasted_iota(jnp.int32, (amp.shape[0], 128), 1)
     marks = jnp.where(spot == 0, owner, 0.0)
     for at, value in ((1, row_hi), (2, row_lo), (3, col_hi), (4, col_lo)):
         marks = jnp.where(spot == at, value, marks)
-    out_ref[:, 4 * half :] = marks.astype(jnp.bfloat16)
+    low_ref[:, 2 * half :] = marks.astype(jnp.bfloat16)
 
 
 MESH = pl.DeviceIdType.MESH
@@ -96,7 +96,7 @@
     wide, narrow, bands, per, meanwhile, amp_ref, par_ref, out_ref, gathered, outgoing, incoming, send_n, recv_n, send_w, recv_w
 ):
     column, band = lax.axis_index("wide"), lax.axis_index("narrow")
-    block = outgoing.shape[1]
+    block = outgoing[0].shape[1]
 
     def first_of(where):
         return jnp.clip(where - REACH, 0, narrow - bands)
@@ -106,39 +106,44 @@
     targets = [((band + d >= 0) & (band + d < narrow), (column, band + d)) for d in deltas]
     peers = [(True, (lax.rem(column + step, wide), band)) for step in range(1, wide)]
     greet(targets + peers)
-    render_into(amp_ref, par_ref, gathered.at[band - first])
-
-    def narrow_copy(k):
+    render_into(amp_ref, par_ref, gathered[0].at[band - first], gathered[1].at[band - first])
+
+    def narrow_copy(part, k):
         there = jnp.clip(band + deltas[k], 0, narrow - 1)
         return pltpu.make_async_remote_copy(
-            src_ref=gathered.at[band - first],
-            dst_ref=gathered.at[jnp.clip(band - first_of(there), 0, bands - 1)],
-            send_sem=send_n.at[k],
-            recv_sem=recv_n.at[k],
+            src_ref=gathered[part].at[band - first],
+            dst_ref=gathered[part].at[jnp.clip(band - first_of(there), 0, bands - 1)],
+            send_sem=send_n.at[part, k],
+            recv_sem=recv_n.at[part, k],
             device_id=(column, there),
             device_id_type=MESH,
         )
 
-    for k in range(len(deltas)):
-
-        @pl.when(targets[k][0])
-        def _(k=k):
-            narrow_copy(k).start()
+    for part in range(2):
+        for k in range(len(deltas)):
+
+            @pl.when(targets[k][0])
+            def _(part=part, k=k):
+                narrow_copy(part, k).start()
 
     for i in range(bands):
         away = first + i - band
 
         @pl.when((away > REACH) | (away < -REACH))
         def _(i=i):
-            gathered[i] = jnp.zeros(gathered.shape[1:], gathered.dtype)
+            for one in gathered:
+                one[i] = jnp.zeros(one.shape[1:], one.dtype)
 
     meanwhile()
-    for k, d in enumerate(deltas):
-
-        @pl.when((band - d >= 0) & (band - d < narrow))
-        def _(k=k):
-            narrow_copy(k).wait_recv()
-
+
+    def narrow_arrive(part):
+        for k, d in enumerate(deltas):
+
+            @pl.when((band - d >= 0) & (band - d < narrow))
+            def _(k=k):
+                narrow_copy(part, k).wait_recv()
+
+    narrow_arrive(0)
     facets = amp_ref.shape[0]
     lane = lax.broadcasted_iota(jnp.int32, (facets, 128), 1)
     below = lax.broadcasted_iota(jnp.int32, (facets, facets), 0) > lax.broadcasted_iota(
@@ -147,52 +152,61 @@
     earlier = jnp.where(below, 1.0, 0.0).astype(jnp.bfloat16)
     select = jnp.where(lax.broadcasted_iota(jnp.int32, (8, 128), 1) == 0, 1.0, 0.0).astype(jnp.bfloat16)
     spot = lax.broadcasted_iota(jnp.int32, (wide * per, facets), 0).astype(jnp.float32)
-    sorted_by_owner = []
+    picks = []
     for i in range(bands):
-        packed = gathered[i]
-        owner = packed[:, 2 * PIXELS :].astype(jnp.float32)[:, 0:1]
+        owner = gathered[0][i][:, PIXELS:].astype(jnp.float32)[:, 0:1]
         chosen = jnp.where(lane.astype(jnp.float32) == owner, 1.0, 0.0)
         rank = jnp.sum(dot(earlier, chosen.astype(jnp.bfloat16)) * chosen, axis=1, keepdims=True)
         slot = jnp.where(lane == 0, owner * float(per) + rank, 0.0).astype(jnp.bfloat16)
         slot = lax.dot_general(
             select, slot, (((1,), (1,)), ((), ())), preferred_element_type=jnp.float32
         )[0:1]
-        pick = jnp.where(spot == slot, 1.0, 0.0).astype(jnp.bfloat16)
-        sorted_by_owner.append(dot(pick, packed))
+        picks.append(jnp.where(spot == slot, 1.0, 0.0).astype(jnp.bfloat16))
     spare = block - bands * per
-    for w in range(wide):
-        pieces = [one[w * per : (w + 1) * per] for one in sorted_by_owner]
-        if spare:
-            pieces.append(jnp.zeros((spare, WORDS), jnp.float32))
-        outgoing[w] = jnp.concatenate(pieces, axis=0).astype(jnp.bfloat16)
-
-    def wide_copy(step):
+
+    def wide_copy(part, step):
         there = lax.rem(column + step, wide)
         return pltpu.make_async_remote_copy(
-            src_ref=outgoing.at[there],
-            dst_ref=incoming.at[column],
-            send_sem=send_w.at[step],
-            recv_sem=recv_w.at[step],
+            src_ref=outgoing[part].at[there],
+            dst_ref=incoming[part].at[column],
+            send_sem=send_w.at[part, step],
+            recv_sem=recv_w.at[part, step],
             device_id=(there, band),
             device_id_type=MESH,
         )
 
-    for step in range(1, wide):
-        wide_copy(step).start()
-    incoming[column] = outgoing[column]
-    for step in range(1, wide):
-        wide_copy(step).wait_recv()
-    blocks = [incoming[w].astype(jnp.float32) for w in range(wide)]
-    for i in range(bands):
-        rows = jnp.concatenate([one[i * per : (i + 1) * per] for one in blocks], axis=0)
-        out_ref[i * wide * per : (i + 1) * wide * per, :] = rows.astype(jnp.bfloat16)
-    for step in range(1, wide):
-        wide_copy(step).wait_send()
-    for k in range(len(deltas)):
-
-        @pl.when(targets[k][0])
-        def _(k=k):
-            narrow_copy(k).wait_send()
+    for part in range(2):
+        if part:
+            narrow_arrive(part)
+        by_owner = [dot(picks[i], gathered[part][i]) for i in range(bands)]
+        for w in range(wide):
+            pieces = [one[w * per : (w + 1) * per] for one in by_owner]
+            if spare:
+                pieces.append(jnp.zeros((spare, PARTS[part]), jnp.float32))
+            outgoing[part][w] = jnp.concatenate(pieces, axis=0).astype(jnp.bfloat16)
+        for step in range(1, wide):
+            wide_copy(part, step).start()
+        incoming[part][column] = outgoing[part][column]
+
+    def arrive(part):
+        for step in range(1, wide):
+            wide_copy(part, step).wait_recv()
+        blocks = [incoming[part][w].astype(jnp.float32) for w in range(wide)]
+        for i in range(bands):
+            rows = jnp.concatenate([one[i * per : (i + 1) * per] for one in blocks], axis=0)
+            out_ref[part][i * wide * per : (i + 1) * wide * per, :] = rows.astype(jnp.bfloat16)
+
+    def finish():
+        for part in range(2):
+            for step in range(1, wide):
+                wide_copy(part, step).wait_send()
+            for k in range(len(deltas)):
+
+                @pl.when(targets[k][0])
+                def _(part=part, k=k):
+                    narrow_copy(part, k).wait_send()
+
+    return arrive, finish
 
 
 def dot(a, b):
@@ -209,16 +223,18 @@
         tile_ref[at] = jnp.where(group == at, 1.0, 0.0).astype(jnp.bfloat16)
 
 
-def forward(bands, slots, here, pay_ref, tile_ref, tab_ref, weight_ref, wide_ref, out_ref, mask, spread, plane, total):
-    half = PIXELS
-    marks = pay_ref[:, 2 * PIXELS :].astype(jnp.float32)
+def forward(bands, slots, here, arrive, pay_ref, tile_ref, tab_ref, weight_ref, wide_ref, out_ref, mask, spread, plane, total):
+    arrive(0)
+    marks = pay_ref[0][:, PIXELS:].astype(jnp.float32)
     col_at = FACET * marks[:, 3:4] + marks[:, 4:5]
     spot = (lax.broadcasted_iota(jnp.int32, mask.shape, 1) % TW).astype(jnp.float32) - col_at
     mask[...] = jnp.where((spot >= 0.0) & (spot < FACET), 1.0, 0.0).astype(jnp.bfloat16)
-    for side in range(2):
-        fields = pay_ref[:, side * half : (side + 1) * half]
-
-        def widen(at, _):
+    for part, side in ((0, 1), (1, 0)):
+        if part:
+            arrive(part)
+        fields = pay_ref[part][:, :PIXELS]
+
+        def widen(at, _, fields=fields, side=side):
             pixels = dot(fields, tile_ref[at]).astype(jnp.bfloat16) * mask[...]
             row = pl.multiple_of((side * (FACET // 2) + at) * slots, slots)
             for b in range(bands):
@@ -232,7 +248,7 @@
     depth = group * slots
     spot = lax.broadcasted_iota(jnp.int32, (TH, depth), 0).astype(jnp.float32)
     for b in range(bands):
-        corner = pay_ref[b * slots : (b + 1) * slots, 2 * PIXELS :]
+        corner = pay_ref[0][b * slots : (b + 1) * slots, PIXELS:]
         row_at = lax.dot_general(
             select, corner, (((1,), (1,)), ((), ())), preferred_element_type=jnp.float32
         )[0:1]
@@ -330,8 +346,8 @@
 def whole_kernel(
     wide, narrow, bands, per,
     amp_ref, par_ref, row_weight, col_weight, fwd_w, inv_w, phase_all, fwd_h_all, inv_h_all, out_ref,
-    gathered, outgoing, incoming, send_n, recv_n, send_w, recv_w,
-    pay, tiles, mask, spread, plane, total, spec,
+    gathered_a, gathered_b, outgoing_a, outgoing_b, incoming_a, incoming_b, send_n, recv_n, send_w, recv_w,
+    pay_a, pay_b, tiles, mask, spread, plane, total, spec,
     parts, focus, back, image, send_a, recv_a, send_b, recv_b,
     phase, fwd_h, inv_h, load,
 ):
@@ -343,14 +359,16 @@
     fetch_inv = pltpu.make_async_copy(inv_h_all, inv_h, load.at[2])
     for one in (fetch_tab, fetch_phase, fetch_inv):
         one.start()
-    front(
-        wide, narrow, bands, per, lambda: fill_tiles(tiles),
-        amp_ref, par_ref, pay, gathered, outgoing, incoming, send_n, recv_n, send_w, recv_w,
+    pay = (pay_a, pay_b)
+    landed, finish = front(
+        wide, narrow, bands, per, lambda: fill_tiles(tiles), amp_ref, par_ref, pay,
+        (gathered_a, gathered_b), (outgoing_a, outgoing_b), (incoming_a, incoming_b),
+        send_n, recv_n, send_w, recv_w,
     )
     fetch_tab.wait()
     here = band - jnp.clip(band - REACH, 0, narrow - bands)
     forward(
-        bands, wide * per, here, pay, tiles, fwd_h, row_weight, fwd_w, spec, mask, spread, plane, total
+        bands, wide * per, here, landed, pay, tiles, fwd_h, row_weight, fwd_w, spec, mask, spread, plane, total
     )
 
     def arrive():
@@ -361,6 +379,7 @@
         wide, arrive, spec, col_weight, phase, inv_w, inv_h, out_ref,
         parts, focus, back, image, send_a, recv_a, send_b, recv_b,
     )
+    finish()
 
 
 def local(amplitude, tilt, owner, row_offset, col_offset):
@@ -391,7 +410,7 @@
         np.concatenate(dft_tables(TH, -1.0), axis=0),
         np.concatenate(dft_tables(TH, 1.0), axis=0),
     ]
-    dma = lambda count: pltpu.SemaphoreType.DMA((count,))
+    dma = lambda *shape: pltpu.SemaphoreType.DMA(shape)
     narrow16 = lambda *shape: pltpu.VMEM(shape, jnp.bfloat16)
     wide32 = lambda *shape: pltpu.VMEM(shape, jnp.float32)
     return pl.pallas_call(
@@ -400,14 +419,14 @@
         in_specs=[pl.BlockSpec(memory_space=pltpu.VMEM)] * 6 + [pl.BlockSpec(memory_space=pl.ANY)] * 3,
         out_specs=pl.BlockSpec(memory_space=pltpu.VMEM),
         scratch_shapes=[
-            narrow16(bands, facets, WORDS),
-            narrow16(wide, block, WORDS),
-            narrow16(wide, block, WORDS),
-            dma(2 * REACH),
-            dma(2 * REACH),
-            dma(wide),
-            dma(wide),
-            narrow16(bands * slots, WORDS),
+            *[narrow16(bands, facets, words) for words in PARTS],
+            *[narrow16(wide, block, words) for words in PARTS],
+            *[narrow16(wide, block, words) for words in PARTS],
+            dma(2, 2 * REACH),
+            dma(2, 2 * REACH),
+            dma(2, wide),
+            dma(2, wide),
+            *[narrow16(bands * slots, words) for words in PARTS],
             narrow16(FACET // 2, PIXELS, 2 * TW),
             narrow16(bands * slots, 2 * TW),
             narrow16(bands, FACET * slots, 2 * TW),

time: 65.1 us -> 60.2 us (0.925)
  Pallas kernels: 59.9 us -> 54.8 us
    pallas_call x1, Pallas kernels: 59.9 us -> 54.8 us  [local(): pl.pallas_call(functools.partial(whole_kernel, wide, narrow, bands, per),...]
where the time goes in v5:
time: 60.2 us; the launch traced here: 59.2 us
  Pallas kernels  54.8 us (91%)
  local copies, waits for them, and re-layouts  4.34 us (7%)
    pallas_call x1, Pallas kernels, local(): pl.pallas_call(functools.partial(whole_kernel, wide, narrow, bands, per),...  54.8 us
    unnamed x9, local copies, waits for them, and re-layouts  3.62 us

profile of v5, /device:TPU:0, one launch (start us, length us, event | category | flops | bytes accessed | tf_op | source)
XLA Modules:
  0.0 59.2 jit_solution(5322531673617137663)
XLA Ops:
  0.0 0.0 copy-start.1
  0.0 0.0 copy-start.2
  0.0 0.0 copy-start.3
  0.0 0.6 %copy-done.1 = s32[64]{0:T(128)S(1)} copy-done((s32[64]{0:T(128)S(1)}, s32[64]{0:T(128)}, u32[]{:S(2)}) %copy-start.1) | copy-done | bytes 280
  0.7 0.0 copy-done.2
  0.7 0.0 copy-done.3
  0.7 0.0 copy-start
  0.7 0.7 %copy-done = f32[3,64]{1,0:T(4,128)S(1)} copy-done((f32[3,64]{1,0:T(4,128)S(1)}, f32[3,64]{1,0:T(4,128)}, u32[]{:S(2)}) %copy-start) | copy-done | bytes 792
  1.4 0.1 copy.17
  1.5 0.6 %pad.4.par_ref = f32[64,8]{1,0:T(8,128)} pad(f32[64,6]{1,0:T(8,128)S(1)} %bitcast.4, f32[]{:T(128)} %constant.16.clone.1), padding=0_0x0_2 | pad | bytes 3588 | tf_op jit(solution)/shard_map/jit(_pad)/pad | solution.py:396
  2.1 54.8 %shard_map.118 = f32[2,512,256]{2,1,0:T(8,128)} custom-call(f32[64,256]{1,0:T(8,128)} %amp_ref.1, f32[64,8]{1,0:T(8,128)} %pad.4.par_ref, f32[512,128]{1,0:T(8,128)} %constant.17.clone.row_weight, f32[8,256]{1,0:T(8,128)} %constant.18.clone.col_weight, bf16[256,512]{1,0:T(8,128)(2,1)} %constant.19.clone.fwd_w, bf16[256,512]{1,0:T(8,128)(2,1)} %constant.20.clone.inv_w, ...), custom_call_target="tpu_custom_call" | custom-call | tf_op jit(solution)/shard_map/pallas_call | solution.py:416
  56.9 2.3 %copy.19 = f32[2,512,256]{2,1,0:T(8,128)} copy(f32[2,512,256]{2,1,0:T(8,128)} %shard_map.118) | data formatting | bytes 2097152
  (2 shorter events, 0.0 us)
Async XLA Ops:
  0.0 0.7 %copy-start.1 = (s32[64]{0:T(128)S(1)}, s32[64]{0:T(128)}, u32[]{:S(2)}) copy-start(s32[64]{0:T(128)} %param.16) | copy-start | bytes 772
  0.0 0.7 %copy-start.2 = (s32[64]{0:T(128)S(1)}, s32[64]{0:T(128)}, u32[]{:S(2)}) copy-start(s32[64]{0:T(128)} %param.15) | copy-start | bytes 772
  0.0 0.7 %copy-start.3 = (s32[64,1]{0,1:T(1,128)S(1)}, s32[64,1]{0,1:T(1,128)}, u32[]{:S(2)}) copy-start(s32[64,1]{0,1:T(1,128)} %param.14) | copy-start | bytes 772
  0.7 0.7 %copy-start = (f32[3,64]{1,0:T(4,128)S(1)}, f32[3,64]{1,0:T(4,128)}, u32[]{:S(2)}) copy-start(f32[3,64]{1,0:T(4,128)} %param.13) | copy-start | bytes 2308

commit v6 on v5

--- a/solution.py
+++ b/solution.py
@@ -223,7 +223,7 @@
         tile_ref[at] = jnp.where(group == at, 1.0, 0.0).astype(jnp.bfloat16)
 
 
-def forward(bands, slots, here, arrive, pay_ref, tile_ref, tab_ref, weight_ref, wide_ref, out_ref, mask, spread, plane, total):
+def forward(bands, slots, here, arrive, ready, pay_ref, tile_ref, tab_ref, weight_ref, wide_ref, out_ref, mask, spread, plane, total):
     arrive(0)
     marks = pay_ref[0][:, PIXELS:].astype(jnp.float32)
     col_at = FACET * marks[:, 3:4] + marks[:, 4:5]
@@ -256,24 +256,31 @@
         for at in range(FACET // group):
             hot = jnp.where(spot == row_at + float(at * group), 1.0, 0.0).astype(jnp.bfloat16)
             part = dot(hot, spread[b, at * depth : (at + 1) * depth, :])
-            plane[...] = part if at == 0 else plane[...] + part
-        place = lax.broadcasted_iota(jnp.int32, weight_ref.shape, 1) - 2 * REACH
-        weight = jnp.sum(jnp.where(place == here - b, weight_ref[...], 0.0), axis=1, keepdims=True)
-        source = plane[...].astype(jnp.bfloat16)
-        for part in range(2):
-            half = slice(part * TH, (part + 1) * TH)
-            rows = weight * dot(tab_ref[half, :], source)
-            total[half, :] = rows if b == 0 else total[half, :] + rows
+            total[...] = part if at == 0 else total[...] + part
+        plane[b] = total[...].astype(jnp.bfloat16)
     scale = 1.0 / math.sqrt(TH * TW)
-    real = (total[:TH, :TW] - total[TH:, TW:]).astype(jnp.bfloat16)
-    imag = (total[:TH, TW:] + total[TH:, :TW]).astype(jnp.bfloat16)
-    by_real, by_imag = dot(real, wide_ref[...]), dot(imag, wide_ref[...])
-    spec_r = (by_real[:, :TW] - by_imag[:, TW:]) * scale
-    spec_i = (by_real[:, TW:] + by_imag[:, :TW]) * scale
     wide, rows = out_ref.shape[0], out_ref.shape[1] // 2
-    for w in range(wide):
-        here = slice(w * rows, (w + 1) * rows)
-        out_ref[w] = jnp.concatenate([spec_r[here], spec_i[here]], axis=0).astype(jnp.bfloat16)
+    chunk = max(rows, TH // 4)
+    for start in range(0, TH, chunk):
+        span = slice(start, start + chunk)
+        table = jnp.concatenate([tab_ref[span, :], tab_ref[TH + start : TH + start + chunk, :]], axis=0)
+        offsets = weight_ref[span, :]
+        place = lax.broadcasted_iota(jnp.int32, offsets.shape, 1) - 2 * REACH
+        both = None
+        for b in range(bands):
+            weight = jnp.sum(jnp.where(place == here - b, offsets, 0.0), axis=1, keepdims=True)
+            term = jnp.concatenate([weight, weight], axis=0) * dot(table, plane[b])
+            both = term if both is None else both + term
+        real = both[:chunk, :TW] - both[chunk:, TW:]
+        imag = both[:chunk, TW:] + both[chunk:, :TW]
+        pair = jnp.concatenate([real, imag], axis=0).astype(jnp.bfloat16)
+        spread_x = dot(pair, wide_ref[...])
+        spec_r = (spread_x[:chunk, :TW] - spread_x[chunk:, TW:]) * scale
+        spec_i = (spread_x[:chunk, TW:] + spread_x[chunk:, :TW]) * scale
+        for w in range(start // rows, (start + chunk) // rows):
+            part = slice(w * rows - start, (w + 1) * rows - start)
+            out_ref[w] = jnp.concatenate([spec_r[part], spec_i[part]], axis=0).astype(jnp.bfloat16)
+            ready(w)
 
 
 def backward(
@@ -300,8 +307,6 @@
     def home_copy(step):
         return copy(step, focus, back, send_b, recv_b)
 
-    for step in range(1, wide):
-        out_copy(step).start()
     parts[column] = spec_ref[column]
     arrive()
     phase_r, phase_i = phase[0], phase[1]
@@ -367,8 +372,23 @@
     )
     fetch_tab.wait()
     here = band - jnp.clip(band - REACH, 0, narrow - bands)
+
+    def ready(w):
+        step = lax.rem(w - column + wide, wide)
+
+        @pl.when(step != 0)
+        def _():
+            pltpu.make_async_remote_copy(
+                src_ref=spec.at[w],
+                dst_ref=parts.at[column],
+                send_sem=send_a.at[step],
+                recv_sem=recv_a.at[step],
+                device_id=(w, band),
+                device_id_type=MESH,
+            ).start()
+
     forward(
-        bands, wide * per, here, landed, pay, tiles, fwd_h, row_weight, fwd_w, spec, mask, spread, plane, total
+        bands, wide * per, here, landed, ready, pay, tiles, fwd_h, row_weight, fwd_w, spec, mask, spread, plane, total
     )
 
     def arrive():
@@ -430,8 +450,8 @@
             narrow16(FACET // 2, PIXELS, 2 * TW),
             narrow16(bands * slots, 2 * TW),
             narrow16(bands, FACET * slots, 2 * TW),
+            narrow16(bands, TH, 2 * TW),
             wide32(TH, 2 * TW),
-            wide32(2 * TH, 2 * TW),
             narrow16(wide, 2 * rows, TW),
             narrow16(wide, 2 * rows, TW),
             narrow16(wide, 2 * rows, TW),

time: 60.2 us -> 60 us (level)
  the two profiles are of different devices: /device:TPU:0 before, /device:TPU:11 now
where the time goes in v6:
time: 60 us; the launch traced here: 59.8 us
  Pallas kernels  55.4 us (92%)
  local copies, waits for them, and re-layouts  4.33 us (7%)
    pallas_call x1, Pallas kernels, local(): pl.pallas_call(functools.partial(whole_kernel, wide, narrow, bands, per),...  55.4 us
    unnamed x9, local copies, waits for them, and re-layouts  3.61 us

profile of v6, /device:TPU:11, one launch (start us, length us, event | category | flops | bytes accessed | tf_op | source)
XLA Modules:
  0.0 59.8 jit_solution(2855118996542677224)
XLA Ops:
  0.0 0.0 copy-start.1
  0.0 0.0 copy-start.2
  0.0 0.0 copy-start.3
  0.0 0.6 %copy-done.1 = s32[64]{0:T(128)S(1)} copy-done((s32[64]{0:T(128)S(1)}, s32[64]{0:T(128)}, u32[]{:S(2)}) %copy-start.1) | copy-done | bytes 280
  0.7 0.0 copy-done.2
  0.7 0.0 copy-done.3
  0.7 0.0 copy-start
  0.7 0.7 %copy-done = f32[3,64]{1,0:T(4,128)S(1)} copy-done((f32[3,64]{1,0:T(4,128)S(1)}, f32[3,64]{1,0:T(4,128)}, u32[]{:S(2)}) %copy-start) | copy-done | bytes 792
  1.4 0.1 copy.17
  1.5 0.6 %pad.4.par_ref = f32[64,8]{1,0:T(8,128)} pad(f32[64,6]{1,0:T(8,128)S(1)} %bitcast.4, f32[]{:T(128)} %constant.16.clone.1), padding=0_0x0_2 | pad | bytes 3588 | tf_op jit(solution)/shard_map/jit(_pad)/pad | solution.py:416
  2.1 55.4 %shard_map.118 = f32[2,512,256]{2,1,0:T(8,128)} custom-call(f32[64,256]{1,0:T(8,128)} %amp_ref.1, f32[64,8]{1,0:T(8,128)} %pad.4.par_ref, f32[512,128]{1,0:T(8,128)} %constant.17.clone.row_weight, f32[8,256]{1,0:T(8,128)} %constant.18.clone.col_weight, bf16[256,512]{1,0:T(8,128)(2,1)} %constant.19.clone.fwd_w, bf16[256,512]{1,0:T(8,128)(2,1)} %constant.20.clone.inv_w, ...), custom_call_target="tpu_custom_call" | custom-call | tf_op jit(solution)/shard_map/pallas_call | solution.py:436
  57.6 2.3 %copy.19 = f32[2,512,256]{2,1,0:T(8,128)} copy(f32[2,512,256]{2,1,0:T(8,128)} %shard_map.118) | data formatting | bytes 2097152
  (2 shorter events, 0.0 us)
Async XLA Ops:
  0.0 0.7 %copy-start.1 = (s32[64]{0:T(128)S(1)}, s32[64]{0:T(128)}, u32[]{:S(2)}) copy-start(s32[64]{0:T(128)} %param.16) | copy-start | bytes 772
  0.0 0.7 %copy-start.2 = (s32[64]{0:T(128)S(1)}, s32[64]{0:T(128)}, u32[]{:S(2)}) copy-start(s32[64]{0:T(128)} %param.15) | copy-start | bytes 772
  0.0 0.7 %copy-start.3 = (s32[64,1]{0,1:T(1,128)S(1)}, s32[64,1]{0,1:T(1,128)}, u32[]{:S(2)}) copy-start(s32[64,1]{0,1:T(1,128)} %param.14) | copy-start | bytes 772
  0.7 0.7 %copy-start = (f32[3,64]{1,0:T(4,128)S(1)}, f32[3,64]{1,0:T(4,128)}, u32[]{:S(2)}) copy-start(f32[3,64]{1,0:T(4,128)} %param.13) | copy-start | bytes 2308
